TPU v7x, 256 devices: a whole 4x4x8 slice. The times are simulated.
256 devices in a mesh: img: 32 (over z_hi, x, core), cls: 8 (over y, z_lo).
Axes of the slice: x: 4, y: 4, z: 8 (z_hi: 4, z_lo: 2; z = z_hi * 2 + z_lo), core: 2. Of those that a mesh axis runs over, the one named last changes fastest.
Arguments:
- images: bfloat16 [2048, 4608], P('img')
- references: bfloat16 [512, 4608], P('cls')
- shifts: int32 [2048, 2], P('img'), may hold values from -4 to 4
- ctf_groups: int32 [2048], P('img'), may hold values from 0 to 15
- ctf_table: float32 [16, 2304], replicated, may hold values from 0.2 to 1
- noise_var: float32 [32], replicated, may hold values from 4 to 16
Outputs:
- class_sums: float32 [512, 4608], P(('cls', 'img'))
- ctf_sums: float32 [512, 2304], P(('cls', 'img'))
- log_evidence: float32 [2048], P('img')
All inputs are finite; a program needn't handle non-finite values.
Results may differ from a plain program's by a relative error of at most 0.013.
Values sent between devices are 32-bit elements; how exact they have to be, the bound alone decides.
No kernel may reach another device: no remote copies, remote signals or barrier semaphores. Data moves between devices by JAX's collectives and lax.ppermute only.
A program may use at most 192 MiB of HBM per device.

v0:
```python
import math

import jax
import jax.numpy as jnp
from jax import lax
from jax.sharding import PartitionSpec as P

ROT = 36
CYCLES = 32
ANG = 72
BOX = 64


highest = lax.Precision.HIGHEST


def polar_frequencies():
    radius = jnp.arange(1, CYCLES + 1, dtype=jnp.float32)
    angle = 2.0 * math.pi * jnp.arange(ANG, dtype=jnp.float32) / ANG
    freq_x = (jnp.cos(angle)[:, None] * radius[None, :]).reshape(-1)
    freq_y = (jnp.sin(angle)[:, None] * radius[None, :]).reshape(-1)
    return (freq_x, freq_y)


def rotate(values, amount, width):
    return jnp.roll(values, amount * width, axis=-1)


def weigh_images(images, shifts, ctf_rows, inverse):
    freq_x, freq_y = polar_frequencies()
    count = images.shape[0]
    grid = images.astype(jnp.float32).reshape(count, ANG, 2, CYCLES)
    real_part = grid[:, :, 0, :].reshape(count, -1)
    imag_part = grid[:, :, 1, :].reshape(count, -1)
    moves = shifts.astype(jnp.float32)
    phase = (
        -2.0 * math.pi / BOX * (moves[:, 0:1] * freq_x[None, :] + moves[:, 1:2] * freq_y[None, :])
    )
    cosine = jnp.cos(phase)
    sine = jnp.sin(phase)
    scale = ctf_rows * inverse[None, :]
    shifted_real = ((real_part * cosine - imag_part * sine) * scale).reshape(count, ANG, CYCLES)
    shifted_imag = ((real_part * sine + imag_part * cosine) * scale).reshape(count, ANG, CYCLES)
    joined = jnp.stack([shifted_real, shifted_imag], axis=2).reshape(count, -1)
    return joined.astype(jnp.bfloat16)


def on_device(images, references, shifts, ctf_groups, ctf_table, noise_var):
    plane = CYCLES * ANG
    classes_dev = references.shape[0]
    group_count = ctf_table.shape[0]
    inverse = jnp.tile(1.0 / noise_var, ANG)
    ctf_weight = ctf_table * ctf_table * inverse[None, :]
    membership = (ctf_groups[:, None] == jnp.arange(group_count, dtype=jnp.int32)[None, :]).astype(
        jnp.float32
    )
    ctf_rows = jnp.dot(membership, ctf_table, precision=highest)
    weighted = weigh_images(images, shifts, ctf_rows, inverse)
    ref_grid = references.astype(jnp.float32).reshape(classes_dev, ANG, 2, CYCLES)
    power = jnp.sum(ref_grid * ref_grid, axis=2).reshape(classes_dev, plane)
    rolled_weight = jnp.stack([rotate(ctf_weight, -2 * turn, CYCLES) for turn in range(ROT)])
    penalty = jnp.einsum("rgp,kp->grk", rolled_weight, power, precision=highest)
    image_penalty = jnp.dot(membership, penalty.reshape(group_count, -1), precision=highest)
    image_penalty = image_penalty.reshape(-1, ROT, classes_dev)
    block = 4
    pieces = []
    for first in range(0, ROT, block):
        bank = jnp.concatenate(
            [rotate(references, 2 * turn, 2 * CYCLES) for turn in range(first, first + block)],
            axis=0,
        )
        product = lax.dot_general(
            weighted, bank, (((1,), (1,)), ((), ())), preferred_element_type=jnp.float32
        )
        pieces.append(product.reshape(-1, block, classes_dev))
    scores = jnp.concatenate(pieces, axis=1) - 0.5 * image_penalty
    local_top = jnp.max(scores, axis=(1, 2))
    local_sum = jnp.sum(jnp.exp(scores - local_top[:, None, None]), axis=(1, 2))
    top = lax.pmax(local_top, "cls")
    total = lax.psum(local_sum * jnp.exp(local_top - top), "cls")
    weights = (jnp.exp(scores - top[:, None, None]) / total[:, None, None]).astype(jnp.bfloat16)
    evidence = top + jnp.log(total)
    group_hot = membership.astype(jnp.bfloat16)
    rows = classes_dev // lax.axis_size("img")
    numerator = jnp.zeros((classes_dev, 2 * plane), jnp.float32)
    for first in range(0, ROT, block):
        image_bank = jnp.stack(
            [rotate(weighted, -2 * turn, 2 * CYCLES) for turn in range(first, first + block)]
        )
        numerator = numerator + jnp.einsum(
            "irk,riq->kq",
            weights[:, first : first + block, :],
            image_bank,
            preferred_element_type=jnp.float32,
        )
    group_weight = jnp.einsum("irk,ig->krg", weights, group_hot, preferred_element_type=jnp.float32)
    tail = jnp.einsum("krg,rgp->kp", group_weight, rolled_weight, precision=highest)
    summed = lax.psum(jnp.concatenate([numerator, tail], axis=1), "img")
    mine = lax.dynamic_slice_in_dim(summed, lax.axis_index("img") * rows, rows, 0)
    denominator = mine[:, 2 * plane :]
    return (mine[:, : 2 * plane], denominator, evidence)


def solution(mesh):
    placed = (P("img", None), P("cls", None), P("img", None), P("img"), P(), P())
    return jax.shard_map(
        on_device,
        mesh=mesh,
        in_specs=placed,
        out_specs=(P(("cls", "img"), None), P(("cls", "img"), None), P("img")),
        check_vma=False,
    )
```

profile of v0, /device:TPU:1, one launch (start us, length us, event | category | flops | bytes accessed | tf_op | source)
XLA Modules:
  0.0 746.7 jit_solution(13047759713135624201)
XLA Ops:
  68.0 2.9 fusion.94
  75.4 4.5 subtract_multiply_fusion
  85.0 3.7 copy.184
  155.8 1.9 copy.194
  157.6 2.1 reduce_sum.18
  159.7 22.1 %stack.284 = f32[36,16,2304]{2,0,1:T(8,128)} concatenate(f32[1,16,2304]{2,0,1:T(1,128)S(1)} %copy.195, f32[1,16,2304]{2,0,1:T(1,128)S(1)} %copy.196, f32[1,16,2304]{2,0,1:T(1,128)S(1)} %copy.197, f32[1,16,2304]{2,0,1:T(1,128)S(1)} %copy.198, f32[1,16,2304]{2,0,1:T(1,128)} %copy.199, f32[1,16,2304]{2,0,1:T(1,128)} %copy.200, f32[1,16,2304]{2,0,1:T(1,128)} %copy.201, ...), dimensions={0} | concatenate | bytes 10616832 | tf_op jit(solution)/shard_map/stack | solution.py:61
  181.9 6.9 convolution_bitcast_fusion.10
  189.1 4.9 maximum_maximum_fusion
  196.3 15.6 %maximum_maximum_fusion.1 = (bf16[256,4608]{1,0:T(8,128)(2,1)S(1)}, bf16[256,4608]{1,0:T(8,128)(2,1)S(1)}) fusion(bf16[64,3712]{1,0:T(8,128)(2,1)S(1)} %copy-done.40, bf16[64,896]{1,0:T(8,128)(2,1)S(1)} %copy-done.150, bf16[64,3840]{1,0:T(8,128)(2,1)S(1)} %copy-done.36, bf16[64,768]{1,0:T(8,128)(2,1)S(1)} %copy-done.162, bf16[64,3968]{1,0:T(8,128)(2,1)S(1)} %copy-done.32, ...), kind=kLoop, calls=%fused_computation.20 | loop fusion | flops 37748736 | bytes 9437184 | tf_op jit(solution)/shard_map/concatenate | solution.py:68
  213.5 8.9 %maximum_maximum_fusion.2 = bf16[256,4608]{1,0:T(8,128)(2,1)S(1)} fusion(bf16[64,3200]{1,0:T(8,128)(2,1)S(1)} %copy-done.54, bf16[64,1408]{1,0:T(8,128)(2,1)S(1)} %copy-done.114, bf16[64,3328]{1,0:T(8,128)(2,1)S(1)} %copy-done.50, bf16[64,1280]{1,0:T(8,128)(2,1)S(1)} %copy-done.118, bf16[64,3456]{1,0:T(8,128)(2,1)S(1)} %copy-done.46, ...), kind=kLoop, calls=%fused_computation.21 | loop fusion | flops 18874368 | bytes 4718592 | tf_op jit(solution)/shard_map/concatenate | solution.py:68
  224.8 21.1 %maximum_maximum_fusion.3 = (bf16[256,4608]{1,0:T(8,128)(2,1)S(1)}, bf16[256,4608]{1,0:T(8,128)(2,1)S(1)}) fusion(bf16[64,2688]{1,0:T(8,128)(2,1)S(1)} %copy-done.70, bf16[64,1920]{1,0:T(8,128)(2,1)S(1)} %copy-done.96, bf16[64,2816]{1,0:T(8,128)(2,1)S(1)} %copy-done.66, bf16[64,1792]{1,0:T(8,128)(2,1)S(1)} %copy-done.100, ...), kind=kLoop, calls=%fused_computation.22 | loop fusion | flops 37748736 | bytes 9437184 | tf_op jit(solution)/shard_map/concatenate | solution.py:68
  247.5 14.4 %maximum_maximum_fusion.4 = bf16[256,4608]{1,0:T(8,128)(2,1)S(1)} fusion(bf16[64,2176]{1,0:T(8,128)(2,1)S(1)} %copy-done.86, bf16[64,2432]{1,0:T(8,128)(2,1)S(1)} %copy-done.78, bf16[64,2304]{1,0:T(8,128)(2,1)S(1)} %copy-done.82, bf16[64,2304]{1,0:T(8,128)(2,1)S(1)} %copy-done.81, bf16[64,2432]{1,0:T(8,128)(2,1)S(1)} %copy-done.77, ...), kind=kLoop, calls=%fused_computation.23 | loop fusion | flops 18874368 | bytes 4718592 | tf_op jit(solution)/shard_map/concatenate | solution.py:68
  264.3 7.8 %maximum_maximum_fusion.6 = bf16[256,4608]{1,0:T(8,128)(2,1)S(1)} fusion(bf16[64,1152]{1,0:T(8,128)(2,1)S(1)} %copy-done.125, bf16[64,3456]{1,0:T(8,128)(2,1)S(1)} %copy-done.45, bf16[64,1280]{1,0:T(8,128)(2,1)S(1)} %copy-done.117, bf16[64,3328]{1,0:T(8,128)(2,1)S(1)} %copy-done.49, bf16[64,1408]{1,0:T(8,128)(2,1)S(1)} %copy-done.113, ...), kind=kLoop, calls=%fused_computation.25 | loop fusion | flops 18874368 | bytes 4718592 | tf_op jit(solution)/shard_map/concatenate | solution.py:68
  275.6 17.5 %pmax.7 = f32[64]{0:T(128)S(1)} all-reduce(f32[64]{0:T(128)S(1)} %get-tuple-element.221), channel_id=1, replica_groups=mesh['img'=32,'cls'=8] {'cls'}, use_global_device_ids=true, to_apply=%region_2.3 | all-reduce | flops 64 | bytes 512 | tf_op jit(solution)/shard_map/pmax | solution.py:79
  293.4 12.8 %psum.14 = f32[64]{0:T(128)S(1)} all-reduce(f32[64]{0:T(128)S(1)} %exponential_multiply_fusion), channel_id=1, replica_groups=mesh['img'=32,'cls'=8] {'cls'}, use_global_device_ids=true, to_apply=%region_4.5 | all-reduce | flops 64 | bytes 512 | tf_op jit(solution)/shard_map/psum | solution.py:80
  306.9 6.9 convolution_bitcast_fusion.9
  315.6 2.3 copy.394
  318.6 2.7 copy.392
  323.9 2.4 copy.388
  327.0 2.3 copy.386
  332.0 2.3 copy.382
  336.0 2.2 copy.380
  341.1 1.9 copy.377
  344.0 1.9 copy.375
  346.9 1.9 copy.373
  349.9 1.9 copy.371
  351.8 2.1 copy.370
  353.9 1.9 copy.369
  356.8 1.9 copy.367
  359.7 2.0 copy.365
  361.7 2.1 copy.364
  363.8 2.0 copy.363
  366.8 2.0 copy.361
  370.7 1.9 copy.358
  372.6 2.1 copy.357
  374.8 1.9 copy.356
  376.7 2.1 copy.355
  378.8 1.9 copy.354
  381.7 1.9 copy.352
  386.4 2.2 copy.349
  390.4 2.2 copy.347
  400.1 2.4 copy.341
  403.3 2.3 copy.339
  406.4 2.4 copy.337
  411.4 2.4 copy.333
  414.5 2.3 copy.331
  417.5 2.3 copy.329
  443.0 293.6 %all-reduce.2.cloned.1.call-done = f32[64,6912]{1,0:T(8,128)} async-done(((f32[64,6912]{1,0:T(8,128)}), f32[64,6912]{1,0:T(8,128)}) %all-reduce.2.cloned.1.call-update) | async-done | bytes 1769488 | tf_op jit(solution)/shard_map/psum | solution.py:98
  (771 shorter events, 216.7 us)
Async XLA Ops:
  7.2 729.4 %all-reduce.2.cloned.1.call-start = ((), (), s32[]{:S(2)}) async-start(), calls=%async_computation | async-start | bytes 3538944 | tf_op jit(solution)/shard_map/psum | solution.py:98
  24.3 11.6 %copy-start = (bf16[64,4608]{1,0:T(8,128)(2,1)S(1)}, bf16[64,4608]{1,0:T(8,128)(2,1)}, u32[]{:S(2)}) copy-start(bf16[64,4608]{1,0:T(8,128)(2,1)} %param.7) | copy-start | bytes 1769476
  128.3 5.5 copy-start.159
  128.3 5.5 copy-start.160
  130.1 5.6 copy-start.165
  130.1 5.5 copy-start.166
  130.2 5.5 copy-start.205
  130.2 5.5 copy-start.206
  141.9 13.0 %copy-start.128 = (f32[16,2240]{1,0:T(8,128)S(1)}, f32[16,2240]{1,0:T(8,128)}, u32[]{:S(2)}) copy-start(f32[16,2240]{1,0:T(8,128)} %get-tuple-element.149) | copy-start | bytes 430084
  141.9 13.0 %copy-start.235 = (f32[16,64]{1,0:T(8,128)S(1)}, f32[16,64]{1,0:T(8,128)}, u32[]{:S(2)}) copy-start(f32[16,64]{1,0:T(8,128)} %get-tuple-element.147) | copy-start | bytes 12292
  181.8 7.2 copy-start.188
  181.8 7.2 copy-start.201
  181.8 7.2 copy-start.202
  181.8 7.2 copy-start.213
  181.8 7.2 copy-start.214
  181.9 7.2 copy-start.227
  181.9 7.2 copy-start.228
  293.0 20.7 %copy-start.238 = (f32[64]{0:T(128)}, f32[64]{0:T(128)S(1)}, u32[]{:S(2)}) copy-start(f32[64]{0:T(128)S(1)} %pmax.7) | copy-start | bytes 772
  306.1 7.6 %copy-start.240 = (f32[64]{0:T(128)}, f32[64]{0:T(128)S(1)}, u32[]{:S(2)}) copy-start(f32[64]{0:T(128)S(1)} %psum.14) | copy-start | bytes 772
  306.9 6.9 copy-start.2
  306.9 8.6 %copy-start.221 = (bf16[64,128]{0,1:T(8,128)(2,1)S(1)}, bf16[64,128]{0,1:T(8,128)(2,1)}, u32[]{:S(2)}) copy-start(bf16[64,128]{0,1:T(8,128)(2,1)} %get-tuple-element.10) | copy-start | bytes 49156
  313.8 7.5 %copy-start.170 = (bf16[64,384]{0,1:T(8,128)(2,1)S(1)}, bf16[64,384]{0,1:T(8,128)(2,1)}, u32[]{:S(2)}) copy-start(bf16[64,384]{0,1:T(8,128)(2,1)} %get-tuple-element.18) | copy-start | bytes 147460
  315.5 6.5 copy-start.3
  315.6 7.6 %copy-start.142 = (bf16[64,512]{0,1:T(8,128)(2,1)S(1)}, bf16[64,512]{0,1:T(8,128)(2,1)}, u32[]{:S(2)}) copy-start(bf16[64,512]{0,1:T(8,128)(2,1)} %get-tuple-element.22) | copy-start | bytes 196612
  318.6 7.6 %copy-start.120 = (bf16[64,640]{0,1:T(8,128)(2,1)S(1)}, bf16[64,640]{0,1:T(8,128)(2,1)}, u32[]{:S(2)}) copy-start(bf16[64,640]{0,1:T(8,128)(2,1)} %get-tuple-element.26) | copy-start | bytes 245764
  322.0 7.3 copy-start.111
  323.1 6.9 copy-start.5
  323.9 7.3 copy-start.98
  331.2 8.9 %copy-start.8 = (bf16[64,3328]{0,1:T(8,128)(2,1)S(1)}, bf16[64,3328]{0,1:T(8,128)(2,1)}, u32[]{:S(2)}) copy-start(bf16[64,3328]{0,1:T(8,128)(2,1)} %get-tuple-element.44) | copy-start | bytes 1277956
  332.0 11.0 %copy-start.9 = (bf16[64,3200]{0,1:T(8,128)(2,1)S(1)}, bf16[64,3200]{0,1:T(8,128)(2,1)}, u32[]{:S(2)}) copy-start(bf16[64,3200]{0,1:T(8,128)(2,1)} %get-tuple-element.48) | copy-start | bytes 1228804
  346.9 8.9 %copy-start.14 = (bf16[64,2688]{0,1:T(8,128)(2,1)S(1)}, bf16[64,2688]{0,1:T(8,128)(2,1)}, u32[]{:S(2)}) copy-start(bf16[64,2688]{0,1:T(8,128)(2,1)} %get-tuple-element.64) | copy-start | bytes 1032196
  349.9 8.9 %copy-start.15 = (bf16[64,2560]{0,1:T(8,128)(2,1)S(1)}, bf16[64,2560]{0,1:T(8,128)(2,1)}, u32[]{:S(2)}) copy-start(bf16[64,2560]{0,1:T(8,128)(2,1)} %get-tuple-element.68) | copy-start | bytes 983044
  359.7 6.1 copy-start.18
  359.7 9.1 %copy-start.21 = (bf16[64,2176]{0,1:T(8,128)(2,1)S(1)}, bf16[64,2176]{0,1:T(8,128)(2,1)}, u32[]{:S(2)}) copy-start(bf16[64,2176]{0,1:T(8,128)(2,1)} %get-tuple-element.73) | copy-start | bytes 835588
  361.7 8.0 %copy-start.16 = (bf16[64,2432]{0,1:T(8,128)(2,1)S(1)}, bf16[64,2432]{0,1:T(8,128)(2,1)}, u32[]{:S(2)}) copy-start(bf16[64,2432]{0,1:T(8,128)(2,1)} %get-tuple-element.71) | copy-start | bytes 933892
  369.7 10.9 %copy-start.13 = (bf16[64,2816]{0,1:T(8,128)(2,1)S(1)}, bf16[64,2816]{0,1:T(8,128)(2,1)}, u32[]{:S(2)}) copy-start(bf16[64,2816]{0,1:T(8,128)(2,1)} %get-tuple-element.59) | copy-start | bytes 1081348
  372.6 10.9 %copy-start.11 = (bf16[64,2944]{0,1:T(8,128)(2,1)S(1)}, bf16[64,2944]{0,1:T(8,128)(2,1)}, u32[]{:S(2)}) copy-start(bf16[64,2944]{0,1:T(8,128)(2,1)} %get-tuple-element.55) | copy-start | bytes 1130500
  383.6 10.9 %copy-start.7 = (bf16[64,3328]{0,1:T(8,128)(2,1)S(1)}, bf16[64,3328]{0,1:T(8,128)(2,1)}, u32[]{:S(2)}) copy-start(bf16[64,3328]{0,1:T(8,128)(2,1)} %get-tuple-element.43) | copy-start | bytes 1277956
  386.4 10.9 %copy-start.6 = (bf16[64,3456]{0,1:T(8,128)(2,1)S(1)}, bf16[64,3456]{0,1:T(8,128)(2,1)}, u32[]{:S(2)}) copy-start(bf16[64,3456]{0,1:T(8,128)(2,1)} %get-tuple-element.39) | copy-start | bytes 1327108
  395.5 7.0 copy-start.97
  397.3 8.3 %copy-start.110 = (bf16[64,768]{0,1:T(8,128)(2,1)S(1)}, bf16[64,768]{0,1:T(8,128)(2,1)}, u32[]{:S(2)}) copy-start(bf16[64,768]{0,1:T(8,128)(2,1)} %get-tuple-element.29) | copy-start | bytes 294916
  400.1 8.6 %copy-start.119 = (bf16[64,640]{0,1:T(8,128)(2,1)S(1)}, bf16[64,640]{0,1:T(8,128)(2,1)}, u32[]{:S(2)}) copy-start(bf16[64,640]{0,1:T(8,128)(2,1)} %get-tuple-element.25) | copy-start | bytes 245764
  400.1 9.4 %copy-start.4 = (bf16[64,3968]{0,1:T(8,128)(2,1)S(1)}, bf16[64,3968]{0,1:T(8,128)(2,1)}, u32[]{:S(2)}) copy-start(bf16[64,3968]{0,1:T(8,128)(2,1)} %get-tuple-element.23) | copy-start | bytes 1523716
  403.3 7.4 copy-start.141
  406.4 7.4 copy-start.169
  409.5 7.2 copy-start.195
  411.4 8.4 %copy-start.220 = (bf16[64,128]{0,1:T(8,128)(2,1)S(1)}, bf16[64,128]{0,1:T(8,128)(2,1)}, u32[]{:S(2)}) copy-start(bf16[64,128]{0,1:T(8,128)(2,1)} %get-tuple-element.9) | copy-start | bytes 49156
  411.4 9.1 %copy-start.1 = (bf16[64,4480]{0,1:T(8,128)(2,1)S(1)}, bf16[64,4480]{0,1:T(8,128)(2,1)}, u32[]{:S(2)}) copy-start(bf16[64,4480]{0,1:T(8,128)(2,1)} %get-tuple-element.7) | copy-start | bytes 1720324
  (195 other events, 453.3 us)
Sparse Core Ops, SparseCore 0:
  442.6 293.9 all-reduce.1
where the time goes:
time: 760 us; the launch traced here: 747 us
  waiting for transfers between devices  294 us (39%)
  local copies, waits for them, and re-layouts  284 us (37%)
  other arithmetic  87.8 us (12%)
  matrix products  34.3 us (5%)
  blocking collectives  30.2 us (4%)
  between operations  16.3 us (2%)
    psum x1, waiting for transfers between devices, on_device(): summed = lax.psum(jnp.concatenate([numerator, tail], axis=1), 'img')  294 us
    unnamed x554, local copies, waits for them, and re-layouts  122 us
    slice x105, local copies, waits for them, and re-layouts, rotate(): return jnp.roll(values, amount * width, axis=-1)  92.8 us
    concatenate x6, other arithmetic, on_device(): jnp.concatenate([rotate(references, 2 * turn, 2 * CYCLES) for turn in ran...  72.7 us
    another operation x37, local copies, waits for them, and re-layouts, on_device(): jnp.stack([rotate(ctf_weight, -2 * turn, CYCLES) for turn in range(ROT)])  48.6 us
    pmax x1, blocking collectives, on_device(): top = lax.pmax(local_top, 'cls')  17.5 us
  transfers between devices with their start and end apart: 1, of which 1 were waited for; matrix products, arithmetic and copies ran while one was open for 0% of the time, Pallas kernels for 0%

commit v1 on v0

v1 whole, which is shorter than its diff:
```python
import math

import jax
import jax.numpy as jnp
import numpy as np
from jax import lax
from jax.experimental import pallas as pl
from jax.experimental.pallas import tpu as pltpu
from jax.sharding import PartitionSpec as P

ROT = 36
CYCLES = 32
ANG = 72
BOX = 64
GROUPS = 16
IMGS = 64
KDEV = 64
FULL = 2 * ANG * CYCLES
PLANE = ANG * CYCLES
STEP = 4
TURNS = ROT // STEP
ROWS = TURNS * KDEV
COLS = STEP * IMGS
PAIRS = FULL // 256
TILES = PLANE // 256
SENT = FULL + 640

f32 = jnp.float32
bf16 = jnp.bfloat16
NT = (((1,), (1,)), ((), ()))
NN = (((1,), (0,)), ((), ()))


def trig_fit():
    grid = 0.5 * np.cos(np.pi * (np.arange(2000) + 0.5) / 2000)
    square = grid * grid
    cosine = np.polynomial.chebyshev.Chebyshev.fit(square, np.cos(2 * np.pi * grid), 6)
    sine = np.polynomial.chebyshev.Chebyshev.fit(square, np.sin(2 * np.pi * grid) / grid, 6)
    to_power = lambda fit: [float(c) for c in fit.convert(kind=np.polynomial.Polynomial).coef]
    return to_power(cosine), to_power(sine)


COS, SIN = trig_fit()


def horner(coefficients, x):
    value = jnp.full_like(x, coefficients[-1])
    for c in coefficients[-2::-1]:
        value = value * x + c
    return value


def split3(x):
    high = x.astype(bf16)
    rest = x - high.astype(f32)
    middle = rest.astype(bf16)
    low = (rest - middle.astype(f32)).astype(bf16)
    return high, middle, low


def dot(a, b, dims):
    return lax.dot_general(a, b, dims, preferred_element_type=f32)


def block(ref, index, count, width=256):
    index = index % count
    return ref[:, index * width : (index + 1) * width]


def image_tile(w_ref, pair):
    rows = []
    for s in range(STEP):
        first = (2 * pair + s) % (2 * PAIRS)
        if first + 1 < 2 * PAIRS:
            rows.append(w_ref[:, first * 128 : first * 128 + 256])
        else:
            rows.append(jnp.concatenate([w_ref[:, first * 128 :], w_ref[:, :128]], axis=1))
    return jnp.concatenate(rows, axis=0)


def group_rows(groups, rows):
    row = lax.broadcasted_iota(jnp.int32, (rows, COLS), 0)
    column = lax.broadcasted_iota(jnp.int32, (rows, COLS), 1)
    wide = jnp.concatenate([groups] * STEP, axis=1)
    same = ((row // GROUPS) % STEP == column // IMGS) & (row % GROUPS == wide)
    return same


def score_kernel(
    place_ref, images_ref, references_ref, shifts_ref, groups_ref, ctf_ref, noise_ref,
    expo_ref, weighted_ref, stats_ref, weight_ref, refs, power_high, power_low,
):
    lane = lax.broadcasted_iota(jnp.int32, (1, 128), 1)
    lane64 = lax.broadcasted_iota(jnp.int32, (64, 128), 1)
    partner = jnp.bitwise_xor(lane64, 32)
    inverse = jnp.concatenate([1.0 / noise_ref[...]] * 4, axis=1)
    groups = groups_ref[...]

    x, z, core = place_ref[0], place_ref[1], place_ref[2]
    out_row = lax.broadcasted_iota(jnp.int32, (KDEV, KDEV), 0)
    in_row = lax.broadcasted_iota(jnp.int32, (KDEV, KDEV), 1)
    to_core = jnp.where(out_row < 32, 1 - core, core)
    to_x = (x + (out_row // 8) % 4) % 4
    to_z = (z + (out_row // 2) % 4) % 4
    order = (in_row == to_z * 16 + to_x * 4 + to_core * 2 + out_row % 2).astype(f32).astype(bf16)
    for pair in range(PAIRS):
        at = slice(pair * 256, (pair + 1) * 256)
        refs[:, at] = dot(order, references_ref[:, at], NN).astype(bf16)

    for tile in range(PAIRS):
        sums = []
        for chunk in (2 * tile, 2 * tile + 1):
            value = refs[:, chunk * 128 : (chunk + 1) * 128].astype(f32)
            value = value * value
            sums.append(value + jnp.take_along_axis(value, partner, axis=1))
        value = jnp.where(
            lane64 < 64, pltpu.roll(sums[0], 96, 1), pltpu.roll(sums[1], 32, 1)
        )
        high = value.astype(bf16)
        at = slice(tile * 128, (tile + 1) * 128)
        power_high[:, at] = high
        power_low[:, at] = (value - high.astype(f32)).astype(bf16)

    plane = [ctf_ref[:, t * 128 : (t + 1) * 128] for t in range(PAIRS)]
    squared = [v * v * inverse for v in plane]
    swapped = [pltpu.roll(v, 64, 1) for v in squared]
    half = lax.broadcasted_iota(jnp.int32, (GROUPS, 128), 1) < 64
    for s in range(STEP):
        for tile in range(PAIRS):
            first = (tile + s // 2) % PAIRS
            if s % 2 == 0:
                value = squared[first]
            else:
                value = jnp.where(half, swapped[first], swapped[(first + 1) % PAIRS])
            for piece, part in enumerate(split3(value)):
                row = piece * STEP * GROUPS + s * GROUPS
                weight_ref[row : row + GROUPS, tile * 128 : (tile + 1) * 128] = part

    row = lax.broadcasted_iota(jnp.int32, (128, 128), 0)
    column = jnp.concatenate([groups, groups], axis=1)
    hot = jnp.where((row % GROUPS == column) & (row < 3 * GROUPS), 1.0, 0.0)
    hot = jnp.transpose(hot)[:IMGS, : 3 * GROUPS].astype(bf16)
    moves = shifts_ref[...].astype(f32)
    move_x = jnp.broadcast_to(moves[:, 0:1], (IMGS, 128))
    move_y = jnp.broadcast_to(moves[:, 1:2], (IMGS, 128))
    radius = (lane % CYCLES + 1).astype(f32) * jnp.where((lane // CYCLES) % 2 == 0, 1.0, -1.0)
    spread = lax.broadcasted_iota(jnp.int32, (GROUPS, 128), 1)
    spread = (spread // 64) * 32 + spread % 32
    for chunk in range(PAIRS):
        angles = [2.0 * math.pi * a / ANG for a in (2 * chunk, 2 * chunk + 1)]
        freq_x = jnp.where(lane < 64, math.cos(angles[0]), math.cos(angles[1])) * radius
        freq_y = jnp.where(lane < 64, math.sin(angles[0]), math.sin(angles[1])) * radius
        turn = move_x * (freq_x * (1.0 / BOX)) + move_y * (freq_y * (1.0 / BOX))
        turn = turn - jnp.round(turn)
        square = turn * turn
        cosine = horner(COS, square)
        sine = horner(SIN, square) * turn
        for at, sign in ((chunk, 1), (chunk + PAIRS, -1)):
            table = plane[at // 2]
            table = jnp.take_along_axis(table, spread + (at % 2) * 64, axis=1)
            scale = dot(hot, jnp.concatenate(split3(table), axis=0), NN) * inverse
            value = images_ref[:, at * 128 : (at + 1) * 128].astype(f32)
            other = jnp.take_along_axis(value, partner, axis=1) * sine
            value = value * cosine
            value = value + other if sign > 0 else value - other
            weighted_ref[:, at * 128 : (at + 1) * 128] = (value * scale).astype(bf16)

    spun = jnp.concatenate(
        [
            jnp.concatenate(
                [block(power_high, t - turn, TILES) for t in range(TILES)]
                + [block(power_low, t - turn, TILES) for t in range(TILES)],
                axis=1,
            )
            for turn in range(TURNS)
        ],
        axis=0,
    )
    by_group = dot(spun, jnp.concatenate([weight_ref[...], weight_ref[...]], axis=1), NT)
    member = jnp.where(group_rows(groups, 3 * STEP * GROUPS), -0.5, 0.0).astype(bf16)
    scores = sum(dot(piece, member, NN) for piece in split3(by_group))

    spun = jnp.concatenate(
        [
            jnp.concatenate([block(refs, t - 2 * turn, PAIRS) for t in range(PAIRS)], axis=1)
            for turn in range(TURNS)
        ],
        axis=0,
    )
    moved = jnp.concatenate([image_tile(weighted_ref, t) for t in range(PAIRS)], axis=1)
    scores = scores + dot(spun, moved, NT)

    def over_turns(value, join):
        value = join(value[:, :128], value[:, 128:])
        value = jnp.broadcast_to(value, (8, 128))
        return join(value, pltpu.roll(value, 64, 1))

    top = over_turns(jnp.max(scores, axis=0, keepdims=True), jnp.maximum)
    expo = jnp.exp(scores - jnp.concatenate([top, top], axis=1)[:1])
    expo_ref[...] = expo
    total = over_turns(jnp.sum(expo, axis=0, keepdims=True), jnp.add)
    for device in range(stats_ref.shape[0]):
        stats_ref[device, 0:1, :] = top[:1]
        stats_ref[device, 1:2, :] = total[:1]


def sum_kernel(
    stats_ref, mine_ref, expo_ref, weighted_ref, groups_ref, keep_ref, send_ref, evidence_ref,
    scaled, sums,
):
    tops = stats_ref[:, 0, :]
    top = jnp.max(tops, axis=0, keepdims=True)
    total = jnp.sum(stats_ref[:, 1, :] * jnp.exp(tops - top), axis=0, keepdims=True)
    evidence_ref[...] = (top + jnp.log(total))[:, :IMGS]
    factor = jnp.exp(mine_ref[0, 0:1, :] - top) / total
    scaled[...] = (expo_ref[...] * jnp.concatenate([factor, factor], axis=1)).astype(bf16)
    weights = scaled[...]
    for pair in range(PAIRS):
        part = dot(weights, image_tile(weighted_ref, pair), NN)
        for turn in range(TURNS):
            to = (pair - 2 * turn) % PAIRS
            at = slice(to * 256, (to + 1) * 256)
            value = part[turn * KDEV : (turn + 1) * KDEV]
            if pair < 2:
                sums[:, at] = value
            else:
                sums[:, at] += value
    send_ref[:, :FULL] = sums[:32]
    keep_ref[:, :FULL] = sums[32:]
    member = group_rows(groups_ref[...], 2 * STEP * GROUPS).astype(f32).astype(bf16)
    counts = dot(weights, member, NT)
    low = lax.broadcasted_iota(jnp.int32, (KDEV, 128), 1) < 64
    for pair in range((TURNS + 1) // 2):
        first = counts[2 * pair * KDEV : (2 * pair + 1) * KDEV]
        if 2 * pair + 1 < TURNS:
            second = counts[(2 * pair + 1) * KDEV : (2 * pair + 2) * KDEV]
        else:
            second = jnp.zeros_like(first)
        value = jnp.where(low, first, second)
        at = slice(FULL + pair * 128, FULL + (pair + 1) * 128)
        send_ref[:, at] = value[:32]
        keep_ref[:, at] = value[32:]


def last_kernel(a_ref, b_ref, c_ref, d_ref, weight_ref, sums_ref, ctf_ref):
    total = (a_ref[...] + b_ref[...]) + (c_ref[...] + d_ref[...])
    sums_ref[...] = total[:, :FULL]
    counts = jnp.concatenate([total[:, FULL:], jnp.zeros((6, SENT - FULL), f32)], axis=0)
    low = lax.broadcasted_iota(jnp.int32, (8, 128), 1) < 64
    rows = []
    for turn in range(TURNS):
        value = counts[:, (turn // 2) * 128 : (turn // 2 + 1) * 128]
        rows.append(jnp.where(low if turn % 2 == 0 else ~low, value, 0.0))
    counts = jnp.concatenate(rows, axis=0)
    counts = jnp.concatenate([counts] * 3, axis=1)
    size = STEP * GROUPS
    weight = jnp.concatenate(
        [weight_ref[(piece // 2) * size : (piece // 2 + 1) * size, :] for piece in range(6)], axis=0
    )
    spread = sum(dot(piece, weight, NN) for piece in split3(counts))
    for tile in range(TILES):
        value = None
        for turn in range(TURNS):
            source = (tile + turn) % TILES
            term = spread[turn * 8 : (turn + 1) * 8, source * 256 : (source + 1) * 256]
            value = term if value is None else value + term
        ctf_ref[:, tile * 256 : (tile + 1) * 256] = value[:2]


LIMIT = pltpu.CompilerParams(vmem_limit_bytes=48 * 1024 * 1024)


def shape(*dims, dtype=f32):
    return jax.ShapeDtypeStruct(dims, dtype)


def on_device(images, references, shifts, ctf_groups, ctf_table, noise_var):
    cls = lax.axis_size("cls")
    me = lax.axis_index("img")
    core, x, z = me % 2, (me // 2) % 4, me // 8
    groups = ctf_groups.reshape(1, -1)
    vmem = pl.BlockSpec(memory_space=pltpu.VMEM)
    place = jnp.stack([x, z, core]).astype(jnp.int32)
    expo, weighted, stats, weight = pl.pallas_call(
        score_kernel,
        out_shape=(
            shape(ROWS, COLS),
            shape(IMGS, FULL, dtype=bf16),
            shape(cls, 2, 128),
            shape(3 * STEP * GROUPS, PLANE, dtype=bf16),
        ),
        in_specs=[pl.BlockSpec(memory_space=pltpu.SMEM)] + [vmem] * 6,
        scratch_shapes=[
            pltpu.VMEM((KDEV, FULL), bf16),
            pltpu.VMEM((KDEV, PLANE), bf16),
            pltpu.VMEM((KDEV, PLANE), bf16),
        ],
        compiler_params=LIMIT,
        name="scores",
    )(place, images, references, shifts, groups, ctf_table, noise_var.reshape(1, -1))
    gathered = lax.all_to_all(stats, "cls", 0, 0)
    keep, send, evidence = pl.pallas_call(
        sum_kernel,
        out_shape=(shape(KDEV // 2, SENT), shape(KDEV // 2, SENT), shape(1, IMGS)),
        scratch_shapes=[pltpu.VMEM((ROWS, COLS), bf16), pltpu.VMEM((KDEV, FULL), f32)],
        compiler_params=LIMIT,
        name="sums",
    )(gathered, stats, expo, weighted, groups)

    count = lax.axis_size("img")
    over_core = [(i, i ^ 1) for i in range(count)]
    half = keep + lax.ppermute(send, "img", over_core)

    def x_step(d):
        return [(i, (i // 8) * 8 + ((i // 2 + d) % 4) * 2 + i % 2) for i in range(count)]

    def z_step(d):
        return [(i, (i + 8 * d) % count) for i in range(count)]

    quarter = half[:8]
    for d in (1, 2, 3):
        quarter = quarter + lax.ppermute(half[8 * d : 8 * d + 8], "img", x_step(d))
    parts = [quarter[:2]]
    for d in (1, 2, 3):
        parts.append(lax.ppermute(quarter[2 * d : 2 * d + 2], "img", z_step(d)))
    class_sums, ctf_sums = pl.pallas_call(
        last_kernel,
        out_shape=(shape(2, FULL), shape(2, PLANE)),
        compiler_params=LIMIT,
        name="ctf",
    )(*parts, weight)
    return class_sums, ctf_sums, evidence.reshape(-1)


def solution(mesh):
    placed = (P("img", None), P("cls", None), P("img", None), P("img"), P(), P())
    return jax.shard_map(
        on_device,
        mesh=mesh,
        in_specs=placed,
        out_specs=(P(("cls", "img"), None), P(("cls", "img"), None), P("img")),
        check_vma=False,
    )
```

time: 760 us -> 57.2 us (0.08)
  the two profiles are of different devices: /device:TPU:1 before, /device:TPU:2 now
where the time goes in v1:
time: 57.2 us; the launch traced here: 56.9 us
  waiting for transfers between devices  14.3 us (25%)
  starting transfers between devices  13.5 us (24%)
  Pallas kernels  11.8 us (21%)
  blocking collectives  11.8 us (21%)
  local copies, waits for them, and re-layouts  4.57 us (8%)
  between operations  0.71 us (1%)
    all_to_all x1, blocking collectives, on_device(): gathered = lax.all_to_all(stats, 'cls', 0, 0)  11.8 us
    ppermute x3, starting transfers between devices, on_device(): parts.append(lax.ppermute(quarter[2 * d:2 * d + 2], 'img', z_step(d)))  9.28 us
    pallas_call x1, Pallas kernels, on_device(): pl.pallas_call(score_kernel, out_shape=(shape(ROWS, COLS), shape(IMGS, FU...  8.05 us
    ppermute x3, waiting for transfers between devices, on_device(): quarter = quarter + lax.ppermute(half[8 * d:8 * d + 8], 'img', x_step(d))  7.62 us
    ppermute x3, waiting for transfers between devices, on_device(): parts.append(lax.ppermute(quarter[2 * d:2 * d + 2], 'img', z_step(d)))  4.58 us
    unnamed x13, local copies, waits for them, and re-layouts  4.48 us
    ppermute x3, starting transfers between devices, on_device(): quarter = quarter + lax.ppermute(half[8 * d:8 * d + 8], 'img', x_step(d))  4.24 us
    ppermute x1, waiting for transfers between devices, on_device(): half = keep + lax.ppermute(send, 'img', over_core)  2.12 us
  transfers between devices with their start and end apart: 7, of which 5 were waited for; matrix products, arithmetic and copies ran while one was open for 0% of the time, Pallas kernels for 0%

profile of v1, /device:TPU:2, one launch (start us, length us, event | category | flops | bytes accessed | tf_op | source)
XLA Modules:
  0.0 56.9 jit_solution(7862501675233962092)
XLA Ops:
  0.7 0.0 copy-start.5
  0.7 0.7 %copy-done.5 = s32[64,2]{0,1:T(2,128)S(1)} copy-done((s32[64,2]{0,1:T(2,128)S(1)}, s32[64,2]{0,1:T(2,128)}, u32[]{:S(2)}) %copy-start.5) | copy-done | bytes 536
  1.4 0.1 copy.9.shifts_ref
  1.4 0.1 pad_add_fusion.place_ref
  1.5 0.0 copy-start.3
  1.5 0.0 copy-start.4
  1.5 0.7 %copy-done.3 = s32[64]{0:T(128)S(1)} copy-done((s32[64]{0:T(128)S(1)}, s32[64]{0:T(128)}, u32[]{:S(2)}) %copy-start.3) | copy-done | bytes 280
  2.2 0.0 copy-done.4
  2.2 0.0 copy-start
  2.2 1.1 %copy-done = bf16[64,4608]{1,0:T(8,128)(2,1)S(1)} copy-done((bf16[64,4608]{1,0:T(8,128)(2,1)S(1)}, bf16[64,4608]{1,0:T(8,128)(2,1)}, u32[]{:S(2)}) %copy-start) | copy-done | bytes 589848
  3.3 0.0 copy-start.1
  3.3 1.1 %copy-done.1 = bf16[64,4608]{1,0:T(8,128)(2,1)S(1)} copy-done((bf16[64,4608]{1,0:T(8,128)(2,1)S(1)}, bf16[64,4608]{1,0:T(8,128)(2,1)}, u32[]{:S(2)}) %copy-start.1) | copy-done | bytes 589848
  4.3 0.0 copy-start.2
  4.3 0.9 %copy-done.2 = f32[16,2304]{1,0:T(8,128)S(1)} copy-done((f32[16,2304]{1,0:T(8,128)S(1)}, f32[16,2304]{1,0:T(8,128)}, u32[]{:S(2)}) %copy-start.2) | copy-done | bytes 147480
  5.2 8.0 %scores.1 = (f32[576,256]{1,0:T(8,128)S(1)}, bf16[64,4608]{1,0:T(8,128)(2,1)S(1)}, f32[8,2,128]{2,1,0:T(2,128)S(1)}, bf16[192,2304]{1,0:T(8,128)(2,1)S(1)}) custom-call(s32[3]{0:T(128)S(1)} %pad_add_fusion.place_ref, bf16[64,4608]{1,0:T(8,128)(2,1)S(1)} %copy-done, bf16[64,4608]{1,0:T(8,128)(2,1)S(1)} %copy-done.1, s32[64,2]{1,0:T(8,128)S(1)} %copy.9.shifts_ref, ...), custom_call_target="tpu_custom_call" | custom-call | tf_op jit(solution)/shard_map/scores/pallas_call | solution.py:284
  13.3 11.8 %all_to_all.5.stats_ref = f32[8,2,128]{2,1,0:T(2,128)S(1)} all-to-all(f32[8,2,128]{2,1,0:T(2,128)S(1)} %get-tuple-element.12.mine_ref), channel_id=1, replica_groups=mesh['img'=32,'cls'=8] {'cls'}, dimensions={0} | all-to-all | bytes 16384 | tf_op jit(solution)/shard_map/all_to_all | solution.py:301
  25.1 2.1 %sums.1 = (f32[32,5248]{1,0:T(8,128)S(1)}, f32[32,5248]{1,0:T(8,128)S(1)}, f32[1,64]{1,0:T(1,128)}) custom-call(f32[8,2,128]{2,1,0:T(2,128)S(1)} %all_to_all.5.stats_ref, f32[8,2,128]{2,1,0:T(2,128)S(1)} %get-tuple-element.12.mine_ref, f32[576,256]{1,0:T(8,128)S(1)} %get-tuple-element.13.expo_ref, bf16[64,4608]{1,0:T(8,128)(2,1)S(1)} %get-tuple-element.14.weighted_ref, ...), custom_call_target="tpu_custom_call" | custom-call | tf_op jit(solution)/shard_map/sums/pallas_call | solution.py:302
  27.1 0.0 collective-permute-start
  27.1 2.1 %collective-permute-done = f32[32,5248]{1,0:T(8,128)S(1)} collective-permute-done((f32[32,5248]{1,0:T(8,128)S(1)}, f32[32,5248]{1,0:T(8,128)S(1)}, u32[]{:S(2)}, u32[]{:S(2)}) %collective-permute-start) | collective-permute-done | bytes 671776 | tf_op jit(solution)/shard_map/ppermute | solution.py:312
  29.3 0.1 add.23
  29.4 1.6 %collective-permute-start.1 = (f32[8,5248]{1,0:T(8,128)S(1)}, f32[8,5248]{1,0:T(8,128)S(1)}, u32[]{:S(2)}, u32[]{:S(2)}) collective-permute-start(f32[8,5248]{1,0:T(8,128)S(1)} %get-tuple-element.21), channel_id=1, source_target_pairs={{0,16},{8,24},{16,32},{24,40},{32,48},{40,56},{48,0},{56,8},{64,80... | collective-permute-start | bytes 503816 | tf_op jit(solution)/shard_map/ppermute | solution.py:322
  31.0 0.5 collective-permute-start.3
  31.5 2.1 %collective-permute-start.2 = (f32[8,5248]{1,0:T(8,128)S(1)}, f32[8,5248]{1,0:T(8,128)S(1)}, u32[]{:S(2)}, u32[]{:S(2)}) collective-permute-start(f32[8,5248]{1,0:T(8,128)S(1)} %get-tuple-element.23), channel_id=1, source_target_pairs={{0,32},{8,40},{16,48},{24,56},{32,0},{40,8},{48,16},{56,24},{64,96... | collective-permute-start | bytes 503816 | tf_op jit(solution)/shard_map/ppermute | solution.py:322
  33.6 2.7 %collective-permute-done.1 = f32[8,5248]{1,0:T(8,128)S(1)} collective-permute-done((f32[8,5248]{1,0:T(8,128)S(1)}, f32[8,5248]{1,0:T(8,128)S(1)}, u32[]{:S(2)}, u32[]{:S(2)}) %collective-permute-start.1) | collective-permute-done | bytes 167968 | tf_op jit(solution)/shard_map/ppermute | solution.py:322
  36.3 1.2 %collective-permute-done.3 = f32[8,5248]{1,0:T(8,128)S(1)} collective-permute-done((f32[8,5248]{1,0:T(8,128)S(1)}, f32[8,5248]{1,0:T(8,128)S(1)}, u32[]{:S(2)}, u32[]{:S(2)}) %collective-permute-start.3) | collective-permute-done | bytes 167968 | tf_op jit(solution)/shard_map/ppermute | solution.py:322
  37.5 3.8 %collective-permute-done.2 = f32[8,5248]{1,0:T(8,128)S(1)} collective-permute-done((f32[8,5248]{1,0:T(8,128)S(1)}, f32[8,5248]{1,0:T(8,128)S(1)}, u32[]{:S(2)}, u32[]{:S(2)}) %collective-permute-start.2) | collective-permute-done | bytes 167968 | tf_op jit(solution)/shard_map/ppermute | solution.py:322
  41.3 0.1 fusion.3
  41.4 5.5 %collective-permute-start.6 = (f32[2,5248]{1,0:T(2,128)S(1)}, f32[2,5248]{1,0:T(2,128)S(1)}, u32[]{:S(2)}, u32[]{:S(2)}) collective-permute-start(f32[2,5248]{1,0:T(2,128)S(1)} %get-tuple-element.24), channel_id=1, source_target_pairs={{0,192},{8,200},{16,208},{24,216},{32,224},{40,232},{48,240},{56,2... | collective-permute-start | bytes 125960 | tf_op jit(solution)/shard_map/ppermute | solution.py:325
  46.8 1.4 %collective-permute-start.5 = (f32[2,5248]{1,0:T(2,128)S(1)}, f32[2,5248]{1,0:T(2,128)S(1)}, u32[]{:S(2)}, u32[]{:S(2)}) collective-permute-start(f32[2,5248]{1,0:T(2,128)S(1)} %get-tuple-element.25), channel_id=1, source_target_pairs={{0,128},{8,136},{16,144},{24,152},{32,160},{40,168},{48,176},{56,1... | collective-permute-start | bytes 125960 | tf_op jit(solution)/shard_map/ppermute | solution.py:325
  48.3 2.4 %collective-permute-start.4 = (f32[2,5248]{1,0:T(2,128)S(1)}, f32[2,5248]{1,0:T(2,128)S(1)}, u32[]{:S(2)}, u32[]{:S(2)}) collective-permute-start(f32[2,5248]{1,0:T(2,128)S(1)} %get-tuple-element.26), channel_id=1, source_target_pairs={{0,64},{8,72},{16,80},{24,88},{32,96},{40,104},{48,112},{56,120},{... | collective-permute-start | bytes 125960 | tf_op jit(solution)/shard_map/ppermute | solution.py:325
  50.7 0.0 collective-permute-done.6.d_ref
  50.7 4.6 %collective-permute-done.5.c_ref = f32[2,5248]{1,0:T(2,128)S(1)} collective-permute-done((f32[2,5248]{1,0:T(2,128)S(1)}, f32[2,5248]{1,0:T(2,128)S(1)}, u32[]{:S(2)}, u32[]{:S(2)}) %collective-permute-start.5) | collective-permute-done | bytes 42016 | tf_op jit(solution)/shard_map/ppermute | solution.py:325
  55.2 0.0 collective-permute-done.4.b_ref
  55.2 1.7 %ctf.1 = (f32[2,4608]{1,0:T(2,128)}, f32[2,2304]{1,0:T(2,128)}) custom-call(f32[2,5248]{1,0:T(2,128)S(1)} %get-tuple-element.27.a_ref, f32[2,5248]{1,0:T(2,128)S(1)} %collective-permute-done.4.b_ref, f32[2,5248]{1,0:T(2,128)S(1)} %collective-permute-done.5.c_ref, f32[2,5248]{1,0:T(2,128)S(1)} %collective-permute-done.6.d_ref, ...), custom_call_target="tpu_custom_call" | custom-call | tf_op jit(solution)/shard_map/ctf/pallas_call | solution.py:326
  (2 shorter events, 0.1 us)
Async XLA Ops:
  0.7 0.7 %copy-start.5 = (s32[64,2]{0,1:T(2,128)S(1)}, s32[64,2]{0,1:T(2,128)}, u32[]{:S(2)}) copy-start(s32[64,2]{0,1:T(2,128)} %param.8) | copy-start | bytes 1540
  1.5 0.7 %copy-start.3 = (s32[64]{0:T(128)S(1)}, s32[64]{0:T(128)}, u32[]{:S(2)}) copy-start(s32[64]{0:T(128)} %param.9) | copy-start | bytes 772
  1.5 0.7 %copy-start.4 = (f32[32]{0:T(128)S(1)}, f32[32]{0:T(128)}, u32[]{:S(2)}) copy-start(f32[32]{0:T(128)} %param.11) | copy-start | bytes 388
  2.2 1.1 %copy-start = (bf16[64,4608]{1,0:T(8,128)(2,1)S(1)}, bf16[64,4608]{1,0:T(8,128)(2,1)}, u32[]{:S(2)}) copy-start(bf16[64,4608]{1,0:T(8,128)(2,1)} %images_ref.1) | copy-start | bytes 1769476
  3.3 1.1 %copy-start.1 = (bf16[64,4608]{1,0:T(8,128)(2,1)S(1)}, bf16[64,4608]{1,0:T(8,128)(2,1)}, u32[]{:S(2)}) copy-start(bf16[64,4608]{1,0:T(8,128)(2,1)} %references_ref.1) | copy-start | bytes 1769476
  4.3 0.9 %copy-start.2 = (f32[16,2304]{1,0:T(8,128)S(1)}, f32[16,2304]{1,0:T(8,128)}, u32[]{:S(2)}) copy-start(f32[16,2304]{1,0:T(8,128)} %ctf_ref.1) | copy-start | bytes 442372
  27.1 2.1 %collective-permute-start = (f32[32,5248]{1,0:T(8,128)S(1)}, f32[32,5248]{1,0:T(8,128)S(1)}, u32[]{:S(2)}, u32[]{:S(2)}) collective-permute-start(f32[32,5248]{1,0:T(8,128)S(1)} %get-tuple-element.16), channel_id=1, source_target_pairs={{0,8},{8,0},{16,24},{24,16},{32,40},{40,32},{48,56},{56,48},{64,72... | collective-permute-start | bytes 2015240 | tf_op jit(solution)/shard_map/ppermute | solution.py:312
  29.4 6.9 %collective-permute-start.1 = (f32[8,5248]{1,0:T(8,128)S(1)}, f32[8,5248]{1,0:T(8,128)S(1)}, u32[]{:S(2)}, u32[]{:S(2)}) collective-permute-start(f32[8,5248]{1,0:T(8,128)S(1)} %get-tuple-element.21), channel_id=1, source_target_pairs={{0,16},{8,24},{16,32},{24,40},{32,48},{40,56},{48,0},{56,8},{64,80... | collective-permute-start | bytes 503816 | tf_op jit(solution)/shard_map/ppermute | solution.py:322
  31.0 6.5 %collective-permute-start.3 = (f32[8,5248]{1,0:T(8,128)S(1)}, f32[8,5248]{1,0:T(8,128)S(1)}, u32[]{:S(2)}, u32[]{:S(2)}) collective-permute-start(f32[8,5248]{1,0:T(8,128)S(1)} %get-tuple-element.22), channel_id=1, source_target_pairs={{0,48},{8,56},{16,0},{24,8},{32,16},{40,24},{48,32},{56,40},{64,11... | collective-permute-start | bytes 503816 | tf_op jit(solution)/shard_map/ppermute | solution.py:322
  31.5 9.8 %collective-permute-start.2 = (f32[8,5248]{1,0:T(8,128)S(1)}, f32[8,5248]{1,0:T(8,128)S(1)}, u32[]{:S(2)}, u32[]{:S(2)}) collective-permute-start(f32[8,5248]{1,0:T(8,128)S(1)} %get-tuple-element.23), channel_id=1, source_target_pairs={{0,32},{8,40},{16,48},{24,56},{32,0},{40,8},{48,16},{56,24},{64,96... | collective-permute-start | bytes 503816 | tf_op jit(solution)/shard_map/ppermute | solution.py:322
  41.4 9.3 %collective-permute-start.6 = (f32[2,5248]{1,0:T(2,128)S(1)}, f32[2,5248]{1,0:T(2,128)S(1)}, u32[]{:S(2)}, u32[]{:S(2)}) collective-permute-start(f32[2,5248]{1,0:T(2,128)S(1)} %get-tuple-element.24), channel_id=1, source_target_pairs={{0,192},{8,200},{16,208},{24,216},{32,224},{40,232},{48,240},{56,2... | collective-permute-start | bytes 125960 | tf_op jit(solution)/shard_map/ppermute | solution.py:325
  46.8 8.4 %collective-permute-start.5 = (f32[2,5248]{1,0:T(2,128)S(1)}, f32[2,5248]{1,0:T(2,128)S(1)}, u32[]{:S(2)}, u32[]{:S(2)}) collective-permute-start(f32[2,5248]{1,0:T(2,128)S(1)} %get-tuple-element.25), channel_id=1, source_target_pairs={{0,128},{8,136},{16,144},{24,152},{32,160},{40,168},{48,176},{56,1... | collective-permute-start | bytes 125960 | tf_op jit(solution)/shard_map/ppermute | solution.py:325
  48.3 6.9 %collective-permute-start.4 = (f32[2,5248]{1,0:T(2,128)S(1)}, f32[2,5248]{1,0:T(2,128)S(1)}, u32[]{:S(2)}, u32[]{:S(2)}) collective-permute-start(f32[2,5248]{1,0:T(2,128)S(1)} %get-tuple-element.26), channel_id=1, source_target_pairs={{0,64},{8,72},{16,80},{24,88},{32,96},{40,104},{48,112},{56,120},{... | collective-permute-start | bytes 125960 | tf_op jit(solution)/shard_map/ppermute | solution.py:325

commit v2 on v1

v2 whole, which is shorter than its diff:
```python
import functools
import math

import jax
import jax.numpy as jnp
import numpy as np
from jax import lax
from jax.experimental import pallas as pl
from jax.experimental.pallas import tpu as pltpu
from jax.sharding import PartitionSpec as P

ROT = 36
CYCLES = 32
ANG = 72
BOX = 64
GROUPS = 16
IMGS = 64
KDEV = 64
FULL = 2 * ANG * CYCLES
PLANE = ANG * CYCLES
STEP = 4
TURNS = ROT // STEP
ROWS = TURNS * KDEV
COLS = STEP * IMGS
PAIRS = FULL // 256
TILES = PLANE // 256
SENT = FULL + 640
WIDE = 12
WIDTH = 256
PARTS = 3

f32 = jnp.float32
bf16 = jnp.bfloat16
NT = (((1,), (1,)), ((), ()))
NN = (((1,), (0,)), ((), ()))


def trig_fit():
    grid = 0.5 * np.cos(np.pi * (np.arange(2000) + 0.5) / 2000)
    square = grid * grid
    cosine = np.polynomial.chebyshev.Chebyshev.fit(square, np.cos(2 * np.pi * grid), 6)
    sine = np.polynomial.chebyshev.Chebyshev.fit(square, np.sin(2 * np.pi * grid) / grid, 6)
    to_power = lambda fit: [float(c) for c in fit.convert(kind=np.polynomial.Polynomial).coef]
    return to_power(cosine), to_power(sine)


COS, SIN = trig_fit()


def horner(coefficients, x):
    value = jnp.full_like(x, coefficients[-1])
    for c in coefficients[-2::-1]:
        value = value * x + c
    return value


def split3(x):
    high = x.astype(bf16)
    rest = x - high.astype(f32)
    middle = rest.astype(bf16)
    low = (rest - middle.astype(f32)).astype(bf16)
    return high, middle, low


def dot(a, b, dims):
    return lax.dot_general(a, b, dims, preferred_element_type=f32)


def block(ref, index, count, width=256):
    index = index % count
    return ref[:, index * width : (index + 1) * width]


def image_tile(w_ref, pair):
    rows = []
    for s in range(STEP):
        first = (2 * pair + s) % (2 * PAIRS)
        if first + 1 < 2 * PAIRS:
            rows.append(w_ref[:, first * 128 : first * 128 + 256])
        else:
            rows.append(jnp.concatenate([w_ref[:, first * 128 :], w_ref[:, :128]], axis=1))
    return jnp.concatenate(rows, axis=0)


def group_rows(groups, rows):
    row = lax.broadcasted_iota(jnp.int32, (rows, COLS), 0)
    column = lax.broadcasted_iota(jnp.int32, (rows, COLS), 1)
    wide = jnp.concatenate([groups] * STEP, axis=1)
    return jnp.where((row & (GROUPS - 1)) == wide, (row >> 4) - (column >> 6), -1)


def score_kernel(
    images_hbm, references_hbm, moves_hbm, groups_hbm, ctf_hbm, noise_hbm,
    expo_ref, weighted_ref, stats_ref, weight_ref, kept_ref,
    images_ref, references_ref, moves_ref, groups_ref, ctf_ref, noise_ref,
    refs, power_high, power_low, wide_high, wide_low, cosines, sines, arrived,
):
    copies = [
        pltpu.make_async_copy(source, target, arrived.at[index])
        for index, (source, target) in enumerate(
            [
                (moves_hbm, moves_ref),
                (groups_hbm, groups_ref),
                (noise_hbm, noise_ref),
                (ctf_hbm, ctf_ref),
                (references_hbm, references_ref),
                (images_hbm, images_ref),
            ]
        )
    ]
    for copy in copies:
        copy.start()

    lane = lax.broadcasted_iota(jnp.int32, (1, 128), 1)
    lane64 = lax.broadcasted_iota(jnp.int32, (64, 128), 1)
    swap = lax.broadcasted_iota(jnp.int32, (256, 256), 0) ^ 32
    swap = swap == lax.broadcasted_iota(jnp.int32, (256, 256), 1)
    swap = jnp.where(swap, 1.0, 0.0).astype(bf16)

    place = lax.axis_index("img")
    core, x, z = lax.rem(place, 2), lax.rem(lax.div(place, 2), 4), lax.div(place, 8)
    out_row = lax.broadcasted_iota(jnp.int32, (KDEV, KDEV), 0)
    in_row = lax.broadcasted_iota(jnp.int32, (KDEV, KDEV), 1)
    to_core = jnp.where(out_row < 32, 1 - core, core)
    to_x = (x + (out_row >> 3)) & 3
    to_z = (z + (out_row >> 1)) & 3
    order = in_row == to_z * 16 + to_x * 4 + to_core * 2 + (out_row & 1)
    order = jnp.where(order, 1.0, 0.0).astype(bf16)

    copies[0].wait()
    copies[1].wait()
    groups = groups_ref[...]
    kept_ref[...] = groups
    row = lax.broadcasted_iota(jnp.int32, (128, 128), 0)
    column = jnp.concatenate([groups, groups], axis=1)
    hot = jnp.where(((row & (GROUPS - 1)) == column) & (row < 3 * GROUPS), 1.0, 0.0)
    moves = jnp.concatenate([moves_ref[...].astype(f32)] * 2, axis=1)
    hot = jnp.where(row == 3 * GROUPS, moves[0:1], hot)
    hot = jnp.where(row == 3 * GROUPS + 1, moves[1:2], hot)
    hot = jnp.transpose(hot)[:IMGS]
    move_x = jnp.broadcast_to(hot[:, 3 * GROUPS : 3 * GROUPS + 1], (IMGS, 128))
    move_y = jnp.broadcast_to(hot[:, 3 * GROUPS + 1 : 3 * GROUPS + 2], (IMGS, 128))
    hot = hot[:, : 3 * GROUPS].astype(bf16)
    radius = ((lane & (CYCLES - 1)) + 1).astype(f32) * jnp.where((lane & CYCLES) == 0, 1.0, -1.0)
    for chunk in range(PAIRS):
        angles = [2.0 * math.pi * a / ANG for a in (2 * chunk, 2 * chunk + 1)]
        freq_x = jnp.where(lane < 64, math.cos(angles[0]), math.cos(angles[1])) * radius
        freq_y = jnp.where(lane < 64, math.sin(angles[0]), math.sin(angles[1])) * radius
        turn = move_x * (freq_x * (1.0 / BOX)) + move_y * (freq_y * (1.0 / BOX))
        turn = turn - jnp.round(turn)
        square = turn * turn
        at = slice(chunk * 128, (chunk + 1) * 128)
        cosines[:, at] = horner(COS, square)
        sines[:, at] = horner(SIN, square) * turn

    copies[2].wait()
    copies[3].wait()
    inverse = jnp.concatenate([1.0 / noise_ref[...]] * 4, axis=1)
    plane = [ctf_ref[:, t * 128 : (t + 1) * 128] for t in range(PAIRS)]
    squared = [v * v * inverse for v in plane]
    swapped = [pltpu.roll(v, 64, 1) for v in squared]
    half = lax.broadcasted_iota(jnp.int32, (GROUPS, 128), 1) < 64
    halfway = [jnp.where(half, swapped[t], swapped[(t + 1) % PAIRS]) for t in range(PAIRS)]
    spare = jnp.zeros((WIDTH - WIDE * GROUPS, PLANE), bf16)
    wide_high[WIDE * GROUPS :, :] = spare
    wide_low[WIDE * GROUPS :, :] = spare
    mixed = lax.broadcasted_iota(jnp.int32, (GROUPS, 128), 1)
    mixed = (mixed & 31) | ((mixed & 32) << 1) | ((mixed & 64) >> 1)
    for odd, values in enumerate((squared, halfway)):
        for tile, value in enumerate(values):
            high = value.astype(bf16)
            low = (value - high.astype(f32)).astype(bf16)
            for s in range(odd, STEP, 2):
                to = (tile - s // 2) % PAIRS
                at = slice(to * 128, (to + 1) * 128)
                weight_ref[s * GROUPS : (s + 1) * GROUPS, at] = high
                weight_ref[(STEP + s) * GROUPS : (STEP + s + 1) * GROUPS, at] = low
            value = jnp.take_along_axis(value, mixed, axis=1)
            high = value.astype(bf16)
            low = (value - high.astype(f32)).astype(bf16)
            for s in range(odd, WIDE, 2):
                to = (tile - s // 2) % PAIRS
                at = slice(to * 128, (to + 1) * 128)
                wide_high[s * GROUPS : (s + 1) * GROUPS, at] = high
                wide_low[s * GROUPS : (s + 1) * GROUPS, at] = low

    copies[4].wait()
    for tile in range(PAIRS):
        at = slice(tile * 256, (tile + 1) * 256)
        value = dot(order, references_ref[:, at], NN)
        refs[:, at] = value.astype(bf16)
        value = value * value
        first, second = value[:, :128], value[:, 128:]
        first = first + pltpu.roll(first, 96, 1)
        second = second + pltpu.roll(second, 32, 1)
        value = jnp.where((lane64 & 32) == 0, first, second)
        high = value.astype(bf16)
        at = slice(tile * 128, (tile + 1) * 128)
        power_high[:, at] = high
        power_low[:, at] = (value - high.astype(f32)).astype(bf16)

    spread = lax.broadcasted_iota(jnp.int32, (GROUPS, 128), 1)
    spread = (spread >> 6) * 32 + (spread & 31)
    def weigh(pair):
        at = slice(pair * 256, (pair + 1) * 256)
        cosine, sine = cosines[:, at], sines[:, at]
        for at, sign in ((pair, 1), (pair + PAIRS // 2, -1)):
            table = plane[at] * inverse
            table = jnp.concatenate(
                [
                    jnp.take_along_axis(table, spread, axis=1),
                    jnp.take_along_axis(table, spread + 64, axis=1),
                ],
                axis=1,
            )
            scale = dot(hot, jnp.concatenate(split3(table), axis=0), NN)
            at = slice(at * 256, (at + 1) * 256)
            value = images_ref[:, at]
            other = dot(value, swap, NN) * sine
            value = value.astype(f32) * cosine
            value = value + other if sign > 0 else value - other
            weighted_ref[:, at] = (value * scale).astype(bf16)

    def spun(ref, count, by, first=0, last=None):
        last = count if last is None else last
        return jnp.concatenate(
            [
                jnp.concatenate(
                    [block(ref, t - turn * by, count) for t in range(first, last)], axis=1
                )
                for turn in range(count // by)
            ],
            axis=0,
        )

    copies[5].wait()
    by_group = None
    for part in range(PARTS):
        first, last = part * TILES // PARTS, (part + 1) * TILES // PARTS
        high = spun(power_high, TILES, 3, first, last)
        low = spun(power_low, TILES, 3, first, last)
        rows = high.shape[0]
        at = slice(first * 256, last * 256)
        both = dot(jnp.concatenate([high, low], axis=0), wide_high[:, at], NT)
        both = (both[:rows] + both[rows:]) + dot(high, wide_low[:, at], NT)
        by_group = both if by_group is None else by_group + both
        for pair in range(first, last):
            weigh(pair)

    pieces = jnp.concatenate(split3(by_group), axis=1)
    penalty = []
    distance = group_rows(groups, WIDTH)
    for first in range(0, WIDE, STEP):
        member = jnp.where(distance == first, -0.5, 0.0).astype(bf16)
        penalty.append(dot(pieces, jnp.concatenate([member] * 3, axis=0), NN))
    count = len(penalty)
    penalty = jnp.concatenate(
        [
            penalty[turn % count][(turn // count) * KDEV : (turn // count + 1) * KDEV]
            for turn in range(TURNS)
        ],
        axis=0,
    )
    moved = jnp.concatenate([image_tile(weighted_ref, t) for t in range(PAIRS)], axis=1)
    scores = dot(spun(refs, PAIRS, 2), moved, NT) + penalty

    def over_turns(value, join):
        value = join(value[:, :128], value[:, 128:])
        value = jnp.broadcast_to(value, (8, 128))
        return join(value, pltpu.roll(value, 64, 1))

    top = over_turns(jnp.max(scores, axis=0, keepdims=True), jnp.maximum)
    expo = jnp.exp(scores - jnp.concatenate([top, top], axis=1)[:1])
    expo_ref[...] = expo
    total = over_turns(jnp.sum(expo, axis=0, keepdims=True), jnp.add)
    for device in range(stats_ref.shape[0]):
        stats_ref[device, 0:1, :] = top[:1]
        stats_ref[device, 1:2, :] = total[:1]


def sum_kernel(first, stats_ref, mine_ref, expo_ref, weighted_ref, groups_ref, out_ref, *rest):
    scaled = rest[-1]
    tops = stats_ref[:, 0, :]
    top = jnp.max(tops, axis=0, keepdims=True)
    total = jnp.sum(stats_ref[:, 1, :] * jnp.exp(tops - top), axis=0, keepdims=True)
    for evidence_ref in rest[:-1]:
        evidence_ref[...] = (top + jnp.log(total))[:, :IMGS]
    factor = jnp.exp(mine_ref[0, 0:1, :] - top) / total
    factor = jnp.concatenate([factor, factor], axis=1)
    half = KDEV // 2
    for turn in range(TURNS):
        source = turn * KDEV + first
        value = expo_ref[source : source + half, :] * factor
        scaled[turn * half : (turn + 1) * half, :] = value.astype(bf16)
    weights = scaled[...]
    for pair in range(PAIRS):
        part = dot(weights, image_tile(weighted_ref, pair), NN)
        for turn in range(TURNS):
            to = (pair - 2 * turn) % PAIRS
            at = slice(to * 256, (to + 1) * 256)
            value = part[turn * half : (turn + 1) * half]
            if pair < 2:
                out_ref[:, at] = value
            else:
                out_ref[:, at] += value
    member = jnp.where(group_rows(groups_ref[...], STEP * GROUPS) == 0, 1.0, 0.0).astype(bf16)
    member = jnp.concatenate([member, member], axis=0)
    counts = dot(weights, member, NT)
    low = lax.broadcasted_iota(jnp.int32, (half, 128), 1) < 64
    for pair in range((TURNS + 1) // 2):
        even = counts[2 * pair * half : (2 * pair + 1) * half]
        if 2 * pair + 1 < TURNS:
            odd = counts[(2 * pair + 1) * half : (2 * pair + 2) * half]
        else:
            odd = jnp.zeros_like(even)
        out_ref[:, FULL + pair * 128 : FULL + (pair + 1) * 128] = jnp.where(low, even, odd)


def last_kernel(a_ref, b_ref, c_ref, d_ref, weight_ref, sums_ref, ctf_ref):
    total = (a_ref[...] + b_ref[...]) + (c_ref[...] + d_ref[...])
    sums_ref[...] = total[:, :FULL]
    counts = jnp.concatenate([total[:, FULL:], jnp.zeros((6, SENT - FULL), f32)], axis=0)
    low = lax.broadcasted_iota(jnp.int32, (8, 128), 1) < 64
    rows = []
    for turn in range(TURNS):
        value = counts[:, (turn // 2) * 128 : (turn // 2 + 1) * 128]
        rows.append(jnp.where(low if turn % 2 == 0 else ~low, value, 0.0))
    counts = jnp.concatenate(rows, axis=0)
    counts = jnp.concatenate([counts] * 2, axis=1)
    high = counts.astype(bf16)
    low = counts - high.astype(f32)
    counts = jnp.concatenate([high.astype(f32), low], axis=0).astype(bf16)
    size = STEP * GROUPS
    weight = jnp.concatenate(
        [weight_ref[(piece // 2) * size : (piece // 2 + 1) * size, :] for piece in range(4)], axis=0
    )
    spread = dot(counts, weight, NN)
    spread = spread[: 8 * TURNS] + spread[8 * TURNS :]
    for tile in range(TILES):
        value = None
        for turn in range(TURNS):
            source = (tile + turn) % TILES
            term = spread[turn * 8 : (turn + 1) * 8, source * 256 : (source + 1) * 256]
            value = term if value is None else value + term
        ctf_ref[:, tile * 256 : (tile + 1) * 256] = value[:2]


LIMIT = pltpu.CompilerParams(vmem_limit_bytes=48 * 1024 * 1024)


def shape(*dims, dtype=f32):
    return jax.ShapeDtypeStruct(dims, dtype)


def on_device(images, references, shifts, ctf_groups, ctf_table, noise_var):
    cls = lax.axis_size("cls")
    groups = ctf_groups.reshape(1, -1)
    inputs = (images, references, shifts.T, groups, ctf_table, noise_var.reshape(1, -1))
    inputs = tuple(pltpu.with_memory_space_constraint(v, pltpu.HBM) for v in inputs)
    expo, weighted, stats, weight, groups = pl.pallas_call(
        score_kernel,
        out_shape=(
            shape(ROWS, COLS),
            shape(IMGS, FULL, dtype=bf16),
            shape(cls, 2, 128),
            shape(2 * STEP * GROUPS, PLANE, dtype=bf16),
            shape(1, IMGS, dtype=jnp.int32),
        ),
        in_specs=[pl.BlockSpec(memory_space=pltpu.HBM)] * 6,
        scratch_shapes=[pltpu.VMEM(value.shape, value.dtype) for value in inputs]
        + [
            pltpu.VMEM((KDEV, FULL), bf16),
            pltpu.VMEM((KDEV, PLANE), bf16),
            pltpu.VMEM((KDEV, PLANE), bf16),
            pltpu.VMEM((WIDTH, PLANE), bf16),
            pltpu.VMEM((WIDTH, PLANE), bf16),
            pltpu.VMEM((IMGS, PLANE), f32),
            pltpu.VMEM((IMGS, PLANE), f32),
            pltpu.SemaphoreType.DMA((6,)),
        ],
        compiler_params=LIMIT,
        name="scores",
    )(*inputs)
    gathered = lax.all_to_all(stats, "cls", 0, 0)
    sums = []
    for first in (0, KDEV // 2):
        evidence = [shape(1, IMGS)] if first else []
        sums += pl.pallas_call(
            functools.partial(sum_kernel, first),
            out_shape=[shape(KDEV // 2, SENT)] + evidence,
            scratch_shapes=[pltpu.VMEM((ROWS // 2, COLS), bf16)],
            compiler_params=LIMIT,
            cost_estimate=pl.CostEstimate(
                flops=ROWS * COLS * FULL, bytes_accessed=2 * ROWS * COLS, transcendentals=0
            ),
            name="sums",
        )(gathered, stats, expo, weighted, groups)
    send, keep, evidence = sums

    count = lax.axis_size("img")
    over_core = [(i, i ^ 1) for i in range(count)]
    half = keep + lax.ppermute(send, "img", over_core)

    def x_step(d):
        return [(i, (i // 8) * 8 + ((i // 2 + d) % 4) * 2 + i % 2) for i in range(count)]

    def z_step(d):
        return [(i, (i + 8 * d) % count) for i in range(count)]

    quarter = half[:8]
    for d in (2, 1, 3):
        quarter = quarter + lax.ppermute(half[8 * d : 8 * d + 8], "img", x_step(d))
    parts = [quarter[:2]]
    for d in (2, 1, 3):
        parts.append(lax.ppermute(quarter[2 * d : 2 * d + 2], "img", z_step(d)))
    class_sums, ctf_sums = pl.pallas_call(
        last_kernel,
        out_shape=(shape(2, FULL), shape(2, PLANE)),
        compiler_params=LIMIT,
        name="ctf",
    )(*parts, weight)
    return class_sums, ctf_sums, evidence.reshape(-1)


def solution(mesh):
    placed = (P("img", None), P("cls", None), P("img", None), P("img"), P(), P())
    return jax.shard_map(
        on_device,
        mesh=mesh,
        in_specs=placed,
        out_specs=(P(("cls", "img"), None), P(("cls", "img"), None), P("img")),
        check_vma=False,
    )
```

time: 57.2 us -> 48.6 us (0.85)
  the two profiles are of different devices: /device:TPU:2 before, /device:TPU:1 now
where the time goes in v2:
time: 48.6 us; the launch traced here: 48.1 us
  starting transfers between devices  14.9 us (31%)
  waiting for transfers between devices  11.3 us (23%)
  blocking collectives  11.2 us (23%)
  Pallas kernels  9.78 us (20%)
  between operations  0.67 us (1%)
    all_to_all x1, blocking collectives, on_device(): gathered = lax.all_to_all(stats, 'cls', 0, 0)  11.2 us
    ppermute x3, starting transfers between devices, on_device(): parts.append(lax.ppermute(quarter[2 * d:2 * d + 2], 'img', z_step(d)))  8.46 us
    pallas_call x1, Pallas kernels, on_device(): pl.pallas_call(score_kernel, out_shape=(shape(ROWS, COLS), shape(IMGS, FU...  6.57 us
    ppermute x3, waiting for transfers between devices, on_device(): quarter = quarter + lax.ppermute(half[8 * d:8 * d + 8], 'img', x_step(d))  6.55 us
    ppermute x3, waiting for transfers between devices, on_device(): parts.append(lax.ppermute(quarter[2 * d:2 * d + 2], 'img', z_step(d)))  4.34 us
    ppermute x3, starting transfers between devices, on_device(): quarter = quarter + lax.ppermute(half[8 * d:8 * d + 8], 'img', x_step(d))  4.3 us
    pallas_call x2, Pallas kernels, on_device(): pl.pallas_call(functools.partial(sum_kernel, first), out_shape=[shape(KDE...  2.24 us
    ppermute x1, starting transfers between devices, on_device(): half = keep + lax.ppermute(send, 'img', over_core)  2.19 us
  transfers between devices with their start and end apart: 7, of which 5 were waited for; matrix products, arithmetic and copies ran while one was open for 0% of the time, Pallas kernels for 3%

profile of v2, /device:TPU:1, one launch (start us, length us, event | category | flops | bytes accessed | tf_op | source)
XLA Modules:
  0.0 48.1 jit_solution(1385050366634871207)
XLA Ops:
  0.6 6.6 %scores.1 = (f32[576,256]{1,0:T(8,128)S(1)}, bf16[64,4608]{1,0:T(8,128)(2,1)S(1)}, f32[8,2,128]{2,1,0:T(2,128)S(1)}, bf16[128,2304]{1,0:T(8,128)(2,1)S(1)}, s32[1,64]{1,0:T(1,128)S(1)}) custom-call(bf16[64,4608]{1,0:T(8,128)(2,1)} %images_hbm.1, bf16[64,4608]{1,0:T(8,128)(2,1)} %references_hbm.1, s32[2,64]{1,0:T(2,128)} %bitcast.4, s32[1,64]{1,0:T(1,128)} %bitcast.5, ...), custom_call_target="tpu_custom_call" | custom-call | tf_op jit(solution)/shard_map/scores/pallas_call | solution.py:360
  7.2 11.2 %all_to_all.5.stats_ref = f32[8,2,128]{2,1,0:T(2,128)S(1)} all-to-all(f32[8,2,128]{2,1,0:T(2,128)S(1)} %get-tuple-element.12.mine_ref), channel_id=1, replica_groups=mesh['img'=32,'cls'=8] {'cls'}, dimensions={0} | all-to-all | bytes 16384 | tf_op jit(solution)/shard_map/all_to_all | solution.py:384
  18.4 0.9 %sums.3 = f32[32,5248]{1,0:T(8,128)S(1)} custom-call(f32[8,2,128]{2,1,0:T(2,128)S(1)} %all_to_all.5.stats_ref, f32[8,2,128]{2,1,0:T(2,128)S(1)} %get-tuple-element.12.mine_ref, f32[576,256]{1,0:T(8,128)S(1)} %get-tuple-element.13.expo_ref, bf16[64,4608]{1,0:T(8,128)(2,1)S(1)} %get-tuple-element.14.weighted_ref, s32[1,64]{1,0:T(1,128)S(1)} %get-tuple-element.15.groups_ref), custom_call_target="tpu_custom_call" | custom-call | flops 679477248 | bytes 294912 | tf_op jit(solution)/shard_map/sums/pallas_call | solution.py:388
  19.3 2.2 %collective-permute-start = (f32[32,5248]{1,0:T(8,128)S(1)}, f32[32,5248]{1,0:T(8,128)S(1)}, u32[]{:S(2)}, u32[]{:S(2)}) collective-permute-start(f32[32,5248]{1,0:T(8,128)S(1)} %sums.3), channel_id=1, source_target_pairs={{0,8},{8,0},{16,24},{24,16},{32,40},{40,32},{48,56},{56,48},{64,72... | collective-permute-start | bytes 2015240 | tf_op jit(solution)/shard_map/ppermute | solution.py:402
  21.5 1.3 %sums.2 = (f32[32,5248]{1,0:T(8,128)S(1)}, f32[1,64]{1,0:T(1,128)}) custom-call(f32[8,2,128]{2,1,0:T(2,128)S(1)} %all_to_all.5.stats_ref, f32[8,2,128]{2,1,0:T(2,128)S(1)} %get-tuple-element.12.mine_ref, f32[576,256]{1,0:T(8,128)S(1)} %get-tuple-element.13.expo_ref, bf16[64,4608]{1,0:T(8,128)(2,1)S(1)} %get-tuple-element.14.weighted_ref, ...), custom_call_target="tpu_custom_call" | custom-call | flops 679477248 | bytes 294912 | tf_op jit(solution)/shard_map/sums/pallas_call | solution.py:388
  22.9 0.4 collective-permute-done
  23.3 0.1 add.12
  23.4 2.8 %collective-permute-start.1 = (f32[8,5248]{1,0:T(8,128)S(1)}, f32[8,5248]{1,0:T(8,128)S(1)}, u32[]{:S(2)}, u32[]{:S(2)}) collective-permute-start(f32[8,5248]{1,0:T(8,128)S(1)} %get-tuple-element.21), channel_id=1, source_target_pairs={{0,32},{8,40},{16,48},{24,56},{32,0},{40,8},{48,16},{56,24},{64,96... | collective-permute-start | bytes 503816 | tf_op jit(solution)/shard_map/ppermute | solution.py:412
  26.2 0.9 %collective-permute-start.3 = (f32[8,5248]{1,0:T(8,128)S(1)}, f32[8,5248]{1,0:T(8,128)S(1)}, u32[]{:S(2)}, u32[]{:S(2)}) collective-permute-start(f32[8,5248]{1,0:T(8,128)S(1)} %get-tuple-element.22), channel_id=1, source_target_pairs={{0,48},{8,56},{16,0},{24,8},{32,16},{40,24},{48,32},{56,40},{64,11... | collective-permute-start | bytes 503816 | tf_op jit(solution)/shard_map/ppermute | solution.py:412
  27.1 0.6 %collective-permute-start.2 = (f32[8,5248]{1,0:T(8,128)S(1)}, f32[8,5248]{1,0:T(8,128)S(1)}, u32[]{:S(2)}, u32[]{:S(2)}) collective-permute-start(f32[8,5248]{1,0:T(8,128)S(1)} %get-tuple-element.23), channel_id=1, source_target_pairs={{0,16},{8,24},{16,32},{24,40},{32,48},{40,56},{48,0},{56,8},{64,80... | collective-permute-start | bytes 503816 | tf_op jit(solution)/shard_map/ppermute | solution.py:412
  27.7 2.8 %collective-permute-done.1 = f32[8,5248]{1,0:T(8,128)S(1)} collective-permute-done((f32[8,5248]{1,0:T(8,128)S(1)}, f32[8,5248]{1,0:T(8,128)S(1)}, u32[]{:S(2)}, u32[]{:S(2)}) %collective-permute-start.1) | collective-permute-done | bytes 167968 | tf_op jit(solution)/shard_map/ppermute | solution.py:412
  30.5 3.7 %collective-permute-done.3 = f32[8,5248]{1,0:T(8,128)S(1)} collective-permute-done((f32[8,5248]{1,0:T(8,128)S(1)}, f32[8,5248]{1,0:T(8,128)S(1)}, u32[]{:S(2)}, u32[]{:S(2)}) %collective-permute-start.3) | collective-permute-done | bytes 167968 | tf_op jit(solution)/shard_map/ppermute | solution.py:412
  34.2 0.0 collective-permute-done.2
  34.3 0.1 fusion.3
  34.4 5.2 %collective-permute-start.6 = (f32[2,5248]{1,0:T(2,128)S(1)}, f32[2,5248]{1,0:T(2,128)S(1)}, u32[]{:S(2)}, u32[]{:S(2)}) collective-permute-start(f32[2,5248]{1,0:T(2,128)S(1)} %get-tuple-element.24), channel_id=1, source_target_pairs={{0,192},{8,200},{16,208},{24,216},{32,224},{40,232},{48,240},{56,2... | collective-permute-start | bytes 125960 | tf_op jit(solution)/shard_map/ppermute | solution.py:415
  39.6 0.0 collective-permute-start.5
  39.6 3.3 %collective-permute-start.4 = (f32[2,5248]{1,0:T(2,128)S(1)}, f32[2,5248]{1,0:T(2,128)S(1)}, u32[]{:S(2)}, u32[]{:S(2)}) collective-permute-start(f32[2,5248]{1,0:T(2,128)S(1)} %get-tuple-element.26), channel_id=1, source_target_pairs={{0,128},{8,136},{16,144},{24,152},{32,160},{40,168},{48,176},{56,1... | collective-permute-start | bytes 125960 | tf_op jit(solution)/shard_map/ppermute | solution.py:415
  42.8 0.0 collective-permute-done.6.d_ref
  42.8 1.7 %collective-permute-done.5.c_ref = f32[2,5248]{1,0:T(2,128)S(1)} collective-permute-done((f32[2,5248]{1,0:T(2,128)S(1)}, f32[2,5248]{1,0:T(2,128)S(1)}, u32[]{:S(2)}, u32[]{:S(2)}) %collective-permute-start.5) | collective-permute-done | bytes 42016 | tf_op jit(solution)/shard_map/ppermute | solution.py:415
  44.5 2.6 %collective-permute-done.4.b_ref = f32[2,5248]{1,0:T(2,128)S(1)} collective-permute-done((f32[2,5248]{1,0:T(2,128)S(1)}, f32[2,5248]{1,0:T(2,128)S(1)}, u32[]{:S(2)}, u32[]{:S(2)}) %collective-permute-start.4) | collective-permute-done | bytes 42016 | tf_op jit(solution)/shard_map/ppermute | solution.py:415
  47.2 1.0 %ctf.1 = (f32[2,4608]{1,0:T(2,128)}, f32[2,2304]{1,0:T(2,128)}) custom-call(f32[2,5248]{1,0:T(2,128)S(1)} %get-tuple-element.27.a_ref, f32[2,5248]{1,0:T(2,128)S(1)} %collective-permute-done.4.b_ref, f32[2,5248]{1,0:T(2,128)S(1)} %collective-permute-done.5.c_ref, f32[2,5248]{1,0:T(2,128)S(1)} %collective-permute-done.6.d_ref, ...), custom_call_target="tpu_custom_call" | custom-call | tf_op jit(solution)/shard_map/ctf/pallas_call | solution.py:416
  (2 shorter events, 0.1 us)
Async XLA Ops:
  19.3 3.9 %collective-permute-start = (f32[32,5248]{1,0:T(8,128)S(1)}, f32[32,5248]{1,0:T(8,128)S(1)}, u32[]{:S(2)}, u32[]{:S(2)}) collective-permute-start(f32[32,5248]{1,0:T(8,128)S(1)} %sums.3), channel_id=1, source_target_pairs={{0,8},{8,0},{16,24},{24,16},{32,40},{40,32},{48,56},{56,48},{64,72... | collective-permute-start | bytes 2015240 | tf_op jit(solution)/shard_map/ppermute | solution.py:402
  23.4 7.1 %collective-permute-start.1 = (f32[8,5248]{1,0:T(8,128)S(1)}, f32[8,5248]{1,0:T(8,128)S(1)}, u32[]{:S(2)}, u32[]{:S(2)}) collective-permute-start(f32[8,5248]{1,0:T(8,128)S(1)} %get-tuple-element.21), channel_id=1, source_target_pairs={{0,32},{8,40},{16,48},{24,56},{32,0},{40,8},{48,16},{56,24},{64,96... | collective-permute-start | bytes 503816 | tf_op jit(solution)/shard_map/ppermute | solution.py:412
  26.2 8.0 %collective-permute-start.3 = (f32[8,5248]{1,0:T(8,128)S(1)}, f32[8,5248]{1,0:T(8,128)S(1)}, u32[]{:S(2)}, u32[]{:S(2)}) collective-permute-start(f32[8,5248]{1,0:T(8,128)S(1)} %get-tuple-element.22), channel_id=1, source_target_pairs={{0,48},{8,56},{16,0},{24,8},{32,16},{40,24},{48,32},{56,40},{64,11... | collective-permute-start | bytes 503816 | tf_op jit(solution)/shard_map/ppermute | solution.py:412
  27.1 7.2 %collective-permute-start.2 = (f32[8,5248]{1,0:T(8,128)S(1)}, f32[8,5248]{1,0:T(8,128)S(1)}, u32[]{:S(2)}, u32[]{:S(2)}) collective-permute-start(f32[8,5248]{1,0:T(8,128)S(1)} %get-tuple-element.23), channel_id=1, source_target_pairs={{0,16},{8,24},{16,32},{24,40},{32,48},{40,56},{48,0},{56,8},{64,80... | collective-permute-start | bytes 503816 | tf_op jit(solution)/shard_map/ppermute | solution.py:412
  34.4 8.5 %collective-permute-start.6 = (f32[2,5248]{1,0:T(2,128)S(1)}, f32[2,5248]{1,0:T(2,128)S(1)}, u32[]{:S(2)}, u32[]{:S(2)}) collective-permute-start(f32[2,5248]{1,0:T(2,128)S(1)} %get-tuple-element.24), channel_id=1, source_target_pairs={{0,192},{8,200},{16,208},{24,216},{32,224},{40,232},{48,240},{56,2... | collective-permute-start | bytes 125960 | tf_op jit(solution)/shard_map/ppermute | solution.py:415
  39.6 5.0 %collective-permute-start.5 = (f32[2,5248]{1,0:T(2,128)S(1)}, f32[2,5248]{1,0:T(2,128)S(1)}, u32[]{:S(2)}, u32[]{:S(2)}) collective-permute-start(f32[2,5248]{1,0:T(2,128)S(1)} %get-tuple-element.25), channel_id=1, source_target_pairs={{0,64},{8,72},{16,80},{24,88},{32,96},{40,104},{48,112},{56,120},{... | collective-permute-start | bytes 125960 | tf_op jit(solution)/shard_map/ppermute | solution.py:415
  39.6 7.6 %collective-permute-start.4 = (f32[2,5248]{1,0:T(2,128)S(1)}, f32[2,5248]{1,0:T(2,128)S(1)}, u32[]{:S(2)}, u32[]{:S(2)}) collective-permute-start(f32[2,5248]{1,0:T(2,128)S(1)} %get-tuple-element.26), channel_id=1, source_target_pairs={{0,128},{8,136},{16,144},{24,152},{32,160},{40,168},{48,176},{56,1... | collective-permute-start | bytes 125960 | tf_op jit(solution)/shard_map/ppermute | solution.py:415

commit v3 on v2

--- a/solution.py
+++ b/solution.py
@@ -122,8 +122,9 @@
     out_row = lax.broadcasted_iota(jnp.int32, (KDEV, KDEV), 0)
     in_row = lax.broadcasted_iota(jnp.int32, (KDEV, KDEV), 1)
     to_core = jnp.where(out_row < 32, 1 - core, core)
-    to_x = (x + (out_row >> 3)) & 3
-    to_z = (z + (out_row >> 1)) & 3
+    near, later = out_row >> 3, out_row >> 1
+    to_x = (x + jnp.where(to_core == 0, near, later)) & 3
+    to_z = (z + jnp.where(to_core == 0, later, near)) & 3
     order = in_row == to_z * 16 + to_x * 4 + to_core * 2 + (out_row & 1)
     order = jnp.where(order, 1.0, 0.0).astype(bf16)
 
@@ -401,18 +402,19 @@
     over_core = [(i, i ^ 1) for i in range(count)]
     half = keep + lax.ppermute(send, "img", over_core)
 
-    def x_step(d):
-        return [(i, (i // 8) * 8 + ((i // 2 + d) % 4) * 2 + i % 2) for i in range(count)]
-
-    def z_step(d):
-        return [(i, (i + 8 * d) % count) for i in range(count)]
+    def step(value, d, stage):
+        pairs = []
+        for i in range(count):
+            along_x = (i // 8) * 8 + ((i // 2 + d) % 4) * 2 + i % 2
+            pairs.append((i, along_x if i % 2 == stage else (i + 8 * d) % count))
+        return lax.ppermute(value, "img", pairs)
 
     quarter = half[:8]
     for d in (2, 1, 3):
-        quarter = quarter + lax.ppermute(half[8 * d : 8 * d + 8], "img", x_step(d))
+        quarter = quarter + step(half[8 * d : 8 * d + 8], d, 0)
     parts = [quarter[:2]]
     for d in (2, 1, 3):
-        parts.append(lax.ppermute(quarter[2 * d : 2 * d + 2], "img", z_step(d)))
+        parts.append(step(quarter[2 * d : 2 * d + 2], d, 1))
     class_sums, ctf_sums = pl.pallas_call(
         last_kernel,
         out_shape=(shape(2, FULL), shape(2, PLANE)),

time: 48.6 us -> 46.9 us (0.965)
  waiting for transfers between devices: 11.3 us -> 9.51 us
  starting transfers between devices: 14.9 us -> 15.4 us
    ppermute x6, waiting for transfers between devices: 10.9 us -> 9.09 us  [step(): return lax.ppermute(value, 'img', pairs)]
  transfers between devices with their start and end apart: 7 -> 7, of which waited for: 5 -> 4; matrix products, arithmetic and copies ran while one was open for 0% -> 0% of each run, Pallas kernels for 3% -> 3%
where the time goes in v3:
time: 46.9 us; the launch traced here: 46.8 us
  starting transfers between devices  15.4 us (33%)
  blocking collectives  11.2 us (24%)
  Pallas kernels  9.78 us (21%)
  waiting for transfers between devices  9.51 us (20%)
  between operations  0.67 us (1%)
    ppermute x6, starting transfers between devices, step(): return lax.ppermute(value, 'img', pairs)  13.2 us
    all_to_all x1, blocking collectives, on_device(): gathered = lax.all_to_all(stats, 'cls', 0, 0)  11.2 us
    ppermute x6, waiting for transfers between devices, step(): return lax.ppermute(value, 'img', pairs)  9.09 us
    pallas_call x1, Pallas kernels, on_device(): pl.pallas_call(score_kernel, out_shape=(shape(ROWS, COLS), shape(IMGS, FU...  6.57 us
    pallas_call x2, Pallas kernels, on_device(): pl.pallas_call(functools.partial(sum_kernel, first), out_shape=[shape(KDE...  2.24 us
    ppermute x1, starting transfers between devices, on_device(): half = keep + lax.ppermute(send, 'img', over_core)  2.19 us
    pallas_call x1, Pallas kernels, on_device(): pl.pallas_call(last_kernel, out_shape=(shape(2, FULL), shape(2, PLANE)),...  0.97 us
  transfers between devices with their start and end apart: 7, of which 4 were waited for; matrix products, arithmetic and copies ran while one was open for 0% of the time, Pallas kernels for 3%

profile of v3, /device:TPU:1, one launch (start us, length us, event | category | flops | bytes accessed | tf_op | source)
XLA Modules:
  0.0 46.8 jit_solution(3584786311144566930)
XLA Ops:
  0.6 6.6 %scores.1 = (f32[576,256]{1,0:T(8,128)S(1)}, bf16[64,4608]{1,0:T(8,128)(2,1)S(1)}, f32[8,2,128]{2,1,0:T(2,128)S(1)}, bf16[128,2304]{1,0:T(8,128)(2,1)S(1)}, s32[1,64]{1,0:T(1,128)S(1)}) custom-call(bf16[64,4608]{1,0:T(8,128)(2,1)} %images_hbm.1, bf16[64,4608]{1,0:T(8,128)(2,1)} %references_hbm.1, s32[2,64]{1,0:T(2,128)} %bitcast.4, s32[1,64]{1,0:T(1,128)} %bitcast.5, ...), custom_call_target="tpu_custom_call" | custom-call | tf_op jit(solution)/shard_map/scores/pallas_call | solution.py:361
  7.2 11.2 %all_to_all.5.stats_ref = f32[8,2,128]{2,1,0:T(2,128)S(1)} all-to-all(f32[8,2,128]{2,1,0:T(2,128)S(1)} %get-tuple-element.12.mine_ref), channel_id=1, replica_groups=mesh['img'=32,'cls'=8] {'cls'}, dimensions={0} | all-to-all | bytes 16384 | tf_op jit(solution)/shard_map/all_to_all | solution.py:385
  18.4 0.9 %sums.3 = f32[32,5248]{1,0:T(8,128)S(1)} custom-call(f32[8,2,128]{2,1,0:T(2,128)S(1)} %all_to_all.5.stats_ref, f32[8,2,128]{2,1,0:T(2,128)S(1)} %get-tuple-element.12.mine_ref, f32[576,256]{1,0:T(8,128)S(1)} %get-tuple-element.13.expo_ref, bf16[64,4608]{1,0:T(8,128)(2,1)S(1)} %get-tuple-element.14.weighted_ref, s32[1,64]{1,0:T(1,128)S(1)} %get-tuple-element.15.groups_ref), custom_call_target="tpu_custom_call" | custom-call | flops 679477248 | bytes 294912 | tf_op jit(solution)/shard_map/sums/pallas_call | solution.py:389
  19.3 2.2 %collective-permute-start = (f32[32,5248]{1,0:T(8,128)S(1)}, f32[32,5248]{1,0:T(8,128)S(1)}, u32[]{:S(2)}, u32[]{:S(2)}) collective-permute-start(f32[32,5248]{1,0:T(8,128)S(1)} %sums.3), channel_id=1, source_target_pairs={{0,8},{8,0},{16,24},{24,16},{32,40},{40,32},{48,56},{56,48},{64,72... | collective-permute-start | bytes 2015240 | tf_op jit(solution)/shard_map/ppermute | solution.py:403
  21.5 1.3 %sums.2 = (f32[32,5248]{1,0:T(8,128)S(1)}, f32[1,64]{1,0:T(1,128)}) custom-call(f32[8,2,128]{2,1,0:T(2,128)S(1)} %all_to_all.5.stats_ref, f32[8,2,128]{2,1,0:T(2,128)S(1)} %get-tuple-element.12.mine_ref, f32[576,256]{1,0:T(8,128)S(1)} %get-tuple-element.13.expo_ref, bf16[64,4608]{1,0:T(8,128)(2,1)S(1)} %get-tuple-element.14.weighted_ref, ...), custom_call_target="tpu_custom_call" | custom-call | flops 679477248 | bytes 294912 | tf_op jit(solution)/shard_map/sums/pallas_call | solution.py:389
  22.9 0.4 collective-permute-done
  23.3 0.1 add.12
  23.4 6.1 %collective-permute-start.1 = (f32[8,5248]{1,0:T(8,128)S(1)}, f32[8,5248]{1,0:T(8,128)S(1)}, u32[]{:S(2)}, u32[]{:S(2)}) collective-permute-start(f32[8,5248]{1,0:T(8,128)S(1)} %get-tuple-element.21), channel_id=1, source_target_pairs={{0,32},{8,136},{16,48},{24,152},{32,0},{40,168},{48,16},{56,184},{... | collective-permute-start | bytes 503816 | tf_op jit(solution)/shard_map/ppermute | solution.py:410
  29.5 0.3 collective-permute-start.3
  29.8 2.1 %collective-permute-start.2 = (f32[8,5248]{1,0:T(8,128)S(1)}, f32[8,5248]{1,0:T(8,128)S(1)}, u32[]{:S(2)}, u32[]{:S(2)}) collective-permute-start(f32[8,5248]{1,0:T(8,128)S(1)} %get-tuple-element.23), channel_id=1, source_target_pairs={{0,16},{8,72},{16,32},{24,88},{32,48},{40,104},{48,0},{56,120},{64... | collective-permute-start | bytes 503816 | tf_op jit(solution)/shard_map/ppermute | solution.py:410
  31.9 0.5 %collective-permute-done.1 = f32[8,5248]{1,0:T(8,128)S(1)} collective-permute-done((f32[8,5248]{1,0:T(8,128)S(1)}, f32[8,5248]{1,0:T(8,128)S(1)}, u32[]{:S(2)}, u32[]{:S(2)}) %collective-permute-start.1) | collective-permute-done | bytes 167968 | tf_op jit(solution)/shard_map/ppermute | solution.py:410
  32.4 5.5 %collective-permute-done.3 = f32[8,5248]{1,0:T(8,128)S(1)} collective-permute-done((f32[8,5248]{1,0:T(8,128)S(1)}, f32[8,5248]{1,0:T(8,128)S(1)}, u32[]{:S(2)}, u32[]{:S(2)}) %collective-permute-start.3) | collective-permute-done | bytes 167968 | tf_op jit(solution)/shard_map/ppermute | solution.py:410
  37.9 0.0 collective-permute-done.2
  37.9 0.1 fusion.3
  38.0 3.0 %collective-permute-start.6 = (f32[2,5248]{1,0:T(2,128)S(1)}, f32[2,5248]{1,0:T(2,128)S(1)}, u32[]{:S(2)}, u32[]{:S(2)}) collective-permute-start(f32[2,5248]{1,0:T(2,128)S(1)} %get-tuple-element.24), channel_id=1, source_target_pairs={{0,192},{8,56},{16,208},{24,8},{32,224},{40,24},{48,240},{56,40},{... | collective-permute-start | bytes 125960 | tf_op jit(solution)/shard_map/ppermute | solution.py:410
  41.0 0.0 collective-permute-start.5
  41.0 1.7 %collective-permute-start.4 = (f32[2,5248]{1,0:T(2,128)S(1)}, f32[2,5248]{1,0:T(2,128)S(1)}, u32[]{:S(2)}, u32[]{:S(2)}) collective-permute-start(f32[2,5248]{1,0:T(2,128)S(1)} %get-tuple-element.26), channel_id=1, source_target_pairs={{0,128},{8,40},{16,144},{24,56},{32,160},{40,8},{48,176},{56,24},{... | collective-permute-start | bytes 125960 | tf_op jit(solution)/shard_map/ppermute | solution.py:410
  42.7 0.0 collective-permute-done.6.d_ref
  42.8 3.1 %collective-permute-done.5.c_ref = f32[2,5248]{1,0:T(2,128)S(1)} collective-permute-done((f32[2,5248]{1,0:T(2,128)S(1)}, f32[2,5248]{1,0:T(2,128)S(1)}, u32[]{:S(2)}, u32[]{:S(2)}) %collective-permute-start.5) | collective-permute-done | bytes 42016 | tf_op jit(solution)/shard_map/ppermute | solution.py:410
  45.8 0.0 collective-permute-done.4.b_ref
  45.8 1.0 %ctf.1 = (f32[2,4608]{1,0:T(2,128)}, f32[2,2304]{1,0:T(2,128)}) custom-call(f32[2,5248]{1,0:T(2,128)S(1)} %get-tuple-element.27.a_ref, f32[2,5248]{1,0:T(2,128)S(1)} %collective-permute-done.4.b_ref, f32[2,5248]{1,0:T(2,128)S(1)} %collective-permute-done.5.c_ref, f32[2,5248]{1,0:T(2,128)S(1)} %collective-permute-done.6.d_ref, ...), custom_call_target="tpu_custom_call" | custom-call | tf_op jit(solution)/shard_map/ctf/pallas_call | solution.py:418
  (2 shorter events, 0.1 us)
Async XLA Ops:
  19.3 3.9 %collective-permute-start = (f32[32,5248]{1,0:T(8,128)S(1)}, f32[32,5248]{1,0:T(8,128)S(1)}, u32[]{:S(2)}, u32[]{:S(2)}) collective-permute-start(f32[32,5248]{1,0:T(8,128)S(1)} %sums.3), channel_id=1, source_target_pairs={{0,8},{8,0},{16,24},{24,16},{32,40},{40,32},{48,56},{56,48},{64,72... | collective-permute-start | bytes 2015240 | tf_op jit(solution)/shard_map/ppermute | solution.py:403
  23.4 9.0 %collective-permute-start.1 = (f32[8,5248]{1,0:T(8,128)S(1)}, f32[8,5248]{1,0:T(8,128)S(1)}, u32[]{:S(2)}, u32[]{:S(2)}) collective-permute-start(f32[8,5248]{1,0:T(8,128)S(1)} %get-tuple-element.21), channel_id=1, source_target_pairs={{0,32},{8,136},{16,48},{24,152},{32,0},{40,168},{48,16},{56,184},{... | collective-permute-start | bytes 503816 | tf_op jit(solution)/shard_map/ppermute | solution.py:410
  29.5 8.4 %collective-permute-start.3 = (f32[8,5248]{1,0:T(8,128)S(1)}, f32[8,5248]{1,0:T(8,128)S(1)}, u32[]{:S(2)}, u32[]{:S(2)}) collective-permute-start(f32[8,5248]{1,0:T(8,128)S(1)} %get-tuple-element.22), channel_id=1, source_target_pairs={{0,48},{8,200},{16,0},{24,216},{32,16},{40,232},{48,32},{56,248},{... | collective-permute-start | bytes 503816 | tf_op jit(solution)/shard_map/ppermute | solution.py:410
  29.8 8.1 %collective-permute-start.2 = (f32[8,5248]{1,0:T(8,128)S(1)}, f32[8,5248]{1,0:T(8,128)S(1)}, u32[]{:S(2)}, u32[]{:S(2)}) collective-permute-start(f32[8,5248]{1,0:T(8,128)S(1)} %get-tuple-element.23), channel_id=1, source_target_pairs={{0,16},{8,72},{16,32},{24,88},{32,48},{40,104},{48,0},{56,120},{64... | collective-permute-start | bytes 503816 | tf_op jit(solution)/shard_map/ppermute | solution.py:410
  38.0 4.8 %collective-permute-start.6 = (f32[2,5248]{1,0:T(2,128)S(1)}, f32[2,5248]{1,0:T(2,128)S(1)}, u32[]{:S(2)}, u32[]{:S(2)}) collective-permute-start(f32[2,5248]{1,0:T(2,128)S(1)} %get-tuple-element.24), channel_id=1, source_target_pairs={{0,192},{8,56},{16,208},{24,8},{32,224},{40,24},{48,240},{56,40},{... | collective-permute-start | bytes 125960 | tf_op jit(solution)/shard_map/ppermute | solution.py:410
  41.0 4.8 %collective-permute-start.5 = (f32[2,5248]{1,0:T(2,128)S(1)}, f32[2,5248]{1,0:T(2,128)S(1)}, u32[]{:S(2)}, u32[]{:S(2)}) collective-permute-start(f32[2,5248]{1,0:T(2,128)S(1)} %get-tuple-element.25), channel_id=1, source_target_pairs={{0,64},{8,24},{16,80},{24,40},{32,96},{40,56},{48,112},{56,8},{64,... | collective-permute-start | bytes 125960 | tf_op jit(solution)/shard_map/ppermute | solution.py:410
  41.0 4.8 %collective-permute-start.4 = (f32[2,5248]{1,0:T(2,128)S(1)}, f32[2,5248]{1,0:T(2,128)S(1)}, u32[]{:S(2)}, u32[]{:S(2)}) collective-permute-start(f32[2,5248]{1,0:T(2,128)S(1)} %get-tuple-element.26), channel_id=1, source_target_pairs={{0,128},{8,40},{16,144},{24,56},{32,160},{40,8},{48,176},{56,24},{... | collective-permute-start | bytes 125960 | tf_op jit(solution)/shard_map/ppermute | solution.py:410

commit v4 on v3

--- a/solution.py
+++ b/solution.py
@@ -138,7 +138,9 @@
     moves = jnp.concatenate([moves_ref[...].astype(f32)] * 2, axis=1)
     hot = jnp.where(row == 3 * GROUPS, moves[0:1], hot)
     hot = jnp.where(row == 3 * GROUPS + 1, moves[1:2], hot)
+    hot = jnp.where(row == 3 * GROUPS + 2, column.astype(f32), hot)
     hot = jnp.transpose(hot)[:IMGS]
+    group_column = hot[:, 3 * GROUPS + 2 : 3 * GROUPS + 3].astype(jnp.int32)
     move_x = jnp.broadcast_to(hot[:, 3 * GROUPS : 3 * GROUPS + 1], (IMGS, 128))
     move_y = jnp.broadcast_to(hot[:, 3 * GROUPS + 1 : 3 * GROUPS + 2], (IMGS, 128))
     hot = hot[:, : 3 * GROUPS].astype(bf16)
@@ -249,21 +251,22 @@
             weigh(pair)
 
     pieces = jnp.concatenate(split3(by_group), axis=1)
-    penalty = []
-    distance = group_rows(groups, WIDTH)
-    for first in range(0, WIDE, STEP):
-        member = jnp.where(distance == first, -0.5, 0.0).astype(bf16)
-        penalty.append(dot(pieces, jnp.concatenate([member] * 3, axis=0), NN))
-    count = len(penalty)
-    penalty = jnp.concatenate(
-        [
-            penalty[turn % count][(turn // count) * KDEV : (turn // count + 1) * KDEV]
-            for turn in range(TURNS)
-        ],
-        axis=0,
-    )
-    moved = jnp.concatenate([image_tile(weighted_ref, t) for t in range(PAIRS)], axis=1)
-    scores = dot(spun(refs, PAIRS, 2), moved, NT) + penalty
+    lane = lax.broadcasted_iota(jnp.int32, (KDEV, pieces.shape[1]), 1)
+    third = (lane >> 6) & 3
+    penalty = [
+        jnp.where(third == turn % 3, pieces[turn // 3 * KDEV : (turn // 3 + 1) * KDEV], 0)
+        for turn in range(TURNS)
+    ]
+    penalty = jnp.concatenate(penalty, axis=0).astype(bf16)
+    lane = lax.broadcasted_iota(jnp.int32, (IMGS, WIDTH), 1)
+    mine = ((lane & (GROUPS - 1)) == group_column) & (lane < WIDE * GROUPS)
+    member = [
+        jnp.where(mine & (((lane >> 4) & 3) == s), -0.5, 0.0).astype(bf16) for s in range(STEP)
+    ]
+    member = jnp.concatenate(member, axis=0)
+    moved = [image_tile(weighted_ref, t) for t in range(PAIRS)]
+    moved = jnp.concatenate(moved + [member] * 3, axis=1)
+    scores = dot(jnp.concatenate([spun(refs, PAIRS, 2), penalty], axis=1), moved, NT)
 
     def over_turns(value, join):
         value = join(value[:, :128], value[:, 128:])

time: 46.9 us -> 46.4 us (0.989)
  Pallas kernels: 9.78 us -> 9.22 us
    pallas_call x1, Pallas kernels: 6.57 us -> 6.02 us  [on_device(): pl.pallas_call(score_kernel, out_shape=(shape(ROWS, COLS), shape(IMGS, FU...]
where the time goes in v4:
time: 46.4 us; the launch traced here: 46.3 us
  starting transfers between devices  15.4 us (33%)
  blocking collectives  11.2 us (24%)
  waiting for transfers between devices  9.51 us (20%)
  Pallas kernels  9.22 us (20%)
  between operations  0.67 us (1%)
    ppermute x6, starting transfers between devices, step(): return lax.ppermute(value, 'img', pairs)  13.2 us
    all_to_all x1, blocking collectives, on_device(): gathered = lax.all_to_all(stats, 'cls', 0, 0)  11.2 us
    ppermute x6, waiting for transfers between devices, step(): return lax.ppermute(value, 'img', pairs)  9.09 us
    pallas_call x1, Pallas kernels, on_device(): pl.pallas_call(score_kernel, out_shape=(shape(ROWS, COLS), shape(IMGS, FU...  6.02 us
    pallas_call x2, Pallas kernels, on_device(): pl.pallas_call(functools.partial(sum_kernel, first), out_shape=[shape(KDE...  2.23 us
    ppermute x1, starting transfers between devices, on_device(): half = keep + lax.ppermute(send, 'img', over_core)  2.2 us
    pallas_call x1, Pallas kernels, on_device(): pl.pallas_call(last_kernel, out_shape=(shape(2, FULL), shape(2, PLANE)),...  0.97 us
  transfers between devices with their start and end apart: 7, of which 4 were waited for; matrix products, arithmetic and copies ran while one was open for 0% of the time, Pallas kernels for 3%

profile of v4, /device:TPU:1, one launch (start us, length us, event | category | flops | bytes accessed | tf_op | source)
XLA Modules:
  0.0 46.3 jit_solution(6459934102508530747)
XLA Ops:
  0.6 6.0 %scores.1 = (f32[576,256]{1,0:T(8,128)S(1)}, bf16[64,4608]{1,0:T(8,128)(2,1)S(1)}, f32[8,2,128]{2,1,0:T(2,128)S(1)}, bf16[128,2304]{1,0:T(8,128)(2,1)S(1)}, s32[1,64]{1,0:T(1,128)S(1)}) custom-call(bf16[64,4608]{1,0:T(8,128)(2,1)} %images_hbm.1, bf16[64,4608]{1,0:T(8,128)(2,1)} %references_hbm.1, s32[2,64]{1,0:T(2,128)} %bitcast.4, s32[1,64]{1,0:T(1,128)} %bitcast.5, ...), custom_call_target="tpu_custom_call" | custom-call | tf_op jit(solution)/shard_map/scores/pallas_call | solution.py:364
  6.7 11.2 %all_to_all.5.stats_ref = f32[8,2,128]{2,1,0:T(2,128)S(1)} all-to-all(f32[8,2,128]{2,1,0:T(2,128)S(1)} %get-tuple-element.12.mine_ref), channel_id=1, replica_groups=mesh['img'=32,'cls'=8] {'cls'}, dimensions={0} | all-to-all | bytes 16384 | tf_op jit(solution)/shard_map/all_to_all | solution.py:388
  17.9 0.9 %sums.3 = f32[32,5248]{1,0:T(8,128)S(1)} custom-call(f32[8,2,128]{2,1,0:T(2,128)S(1)} %all_to_all.5.stats_ref, f32[8,2,128]{2,1,0:T(2,128)S(1)} %get-tuple-element.12.mine_ref, f32[576,256]{1,0:T(8,128)S(1)} %get-tuple-element.13.expo_ref, bf16[64,4608]{1,0:T(8,128)(2,1)S(1)} %get-tuple-element.14.weighted_ref, s32[1,64]{1,0:T(1,128)S(1)} %get-tuple-element.15.groups_ref), custom_call_target="tpu_custom_call" | custom-call | flops 679477248 | bytes 294912 | tf_op jit(solution)/shard_map/sums/pallas_call | solution.py:392
  18.8 2.2 %collective-permute-start = (f32[32,5248]{1,0:T(8,128)S(1)}, f32[32,5248]{1,0:T(8,128)S(1)}, u32[]{:S(2)}, u32[]{:S(2)}) collective-permute-start(f32[32,5248]{1,0:T(8,128)S(1)} %sums.3), channel_id=1, source_target_pairs={{0,8},{8,0},{16,24},{24,16},{32,40},{40,32},{48,56},{56,48},{64,72... | collective-permute-start | bytes 2015240 | tf_op jit(solution)/shard_map/ppermute | solution.py:406
  21.0 1.3 %sums.2 = (f32[32,5248]{1,0:T(8,128)S(1)}, f32[1,64]{1,0:T(1,128)}) custom-call(f32[8,2,128]{2,1,0:T(2,128)S(1)} %all_to_all.5.stats_ref, f32[8,2,128]{2,1,0:T(2,128)S(1)} %get-tuple-element.12.mine_ref, f32[576,256]{1,0:T(8,128)S(1)} %get-tuple-element.13.expo_ref, bf16[64,4608]{1,0:T(8,128)(2,1)S(1)} %get-tuple-element.14.weighted_ref, ...), custom_call_target="tpu_custom_call" | custom-call | flops 679477248 | bytes 294912 | tf_op jit(solution)/shard_map/sums/pallas_call | solution.py:392
  22.3 0.4 collective-permute-done
  22.7 0.1 add.12
  22.9 6.1 %collective-permute-start.1 = (f32[8,5248]{1,0:T(8,128)S(1)}, f32[8,5248]{1,0:T(8,128)S(1)}, u32[]{:S(2)}, u32[]{:S(2)}) collective-permute-start(f32[8,5248]{1,0:T(8,128)S(1)} %get-tuple-element.21), channel_id=1, source_target_pairs={{0,32},{8,136},{16,48},{24,152},{32,0},{40,168},{48,16},{56,184},{... | collective-permute-start | bytes 503816 | tf_op jit(solution)/shard_map/ppermute | solution.py:413
  29.0 0.3 collective-permute-start.3
  29.2 2.1 %collective-permute-start.2 = (f32[8,5248]{1,0:T(8,128)S(1)}, f32[8,5248]{1,0:T(8,128)S(1)}, u32[]{:S(2)}, u32[]{:S(2)}) collective-permute-start(f32[8,5248]{1,0:T(8,128)S(1)} %get-tuple-element.23), channel_id=1, source_target_pairs={{0,16},{8,72},{16,32},{24,88},{32,48},{40,104},{48,0},{56,120},{64... | collective-permute-start | bytes 503816 | tf_op jit(solution)/shard_map/ppermute | solution.py:413
  31.3 0.5 %collective-permute-done.1 = f32[8,5248]{1,0:T(8,128)S(1)} collective-permute-done((f32[8,5248]{1,0:T(8,128)S(1)}, f32[8,5248]{1,0:T(8,128)S(1)}, u32[]{:S(2)}, u32[]{:S(2)}) %collective-permute-start.1) | collective-permute-done | bytes 167968 | tf_op jit(solution)/shard_map/ppermute | solution.py:413
  31.8 5.5 %collective-permute-done.3 = f32[8,5248]{1,0:T(8,128)S(1)} collective-permute-done((f32[8,5248]{1,0:T(8,128)S(1)}, f32[8,5248]{1,0:T(8,128)S(1)}, u32[]{:S(2)}, u32[]{:S(2)}) %collective-permute-start.3) | collective-permute-done | bytes 167968 | tf_op jit(solution)/shard_map/ppermute | solution.py:413
  37.3 0.0 collective-permute-done.2
  37.4 0.1 fusion.3
  37.4 3.0 %collective-permute-start.6 = (f32[2,5248]{1,0:T(2,128)S(1)}, f32[2,5248]{1,0:T(2,128)S(1)}, u32[]{:S(2)}, u32[]{:S(2)}) collective-permute-start(f32[2,5248]{1,0:T(2,128)S(1)} %get-tuple-element.24), channel_id=1, source_target_pairs={{0,192},{8,56},{16,208},{24,8},{32,224},{40,24},{48,240},{56,40},{... | collective-permute-start | bytes 125960 | tf_op jit(solution)/shard_map/ppermute | solution.py:413
  40.5 0.0 collective-permute-start.5
  40.5 1.7 %collective-permute-start.4 = (f32[2,5248]{1,0:T(2,128)S(1)}, f32[2,5248]{1,0:T(2,128)S(1)}, u32[]{:S(2)}, u32[]{:S(2)}) collective-permute-start(f32[2,5248]{1,0:T(2,128)S(1)} %get-tuple-element.26), channel_id=1, source_target_pairs={{0,128},{8,40},{16,144},{24,56},{32,160},{40,8},{48,176},{56,24},{... | collective-permute-start | bytes 125960 | tf_op jit(solution)/shard_map/ppermute | solution.py:413
  42.2 0.0 collective-permute-done.6.d_ref
  42.2 3.1 %collective-permute-done.5.c_ref = f32[2,5248]{1,0:T(2,128)S(1)} collective-permute-done((f32[2,5248]{1,0:T(2,128)S(1)}, f32[2,5248]{1,0:T(2,128)S(1)}, u32[]{:S(2)}, u32[]{:S(2)}) %collective-permute-start.5) | collective-permute-done | bytes 42016 | tf_op jit(solution)/shard_map/ppermute | solution.py:413
  45.3 0.0 collective-permute-done.4.b_ref
  45.3 1.0 %ctf.1 = (f32[2,4608]{1,0:T(2,128)}, f32[2,2304]{1,0:T(2,128)}) custom-call(f32[2,5248]{1,0:T(2,128)S(1)} %get-tuple-element.27.a_ref, f32[2,5248]{1,0:T(2,128)S(1)} %collective-permute-done.4.b_ref, f32[2,5248]{1,0:T(2,128)S(1)} %collective-permute-done.5.c_ref, f32[2,5248]{1,0:T(2,128)S(1)} %collective-permute-done.6.d_ref, ...), custom_call_target="tpu_custom_call" | custom-call | tf_op jit(solution)/shard_map/ctf/pallas_call | solution.py:421
  (2 shorter events, 0.1 us)
Async XLA Ops:
  18.8 3.9 %collective-permute-start = (f32[32,5248]{1,0:T(8,128)S(1)}, f32[32,5248]{1,0:T(8,128)S(1)}, u32[]{:S(2)}, u32[]{:S(2)}) collective-permute-start(f32[32,5248]{1,0:T(8,128)S(1)} %sums.3), channel_id=1, source_target_pairs={{0,8},{8,0},{16,24},{24,16},{32,40},{40,32},{48,56},{56,48},{64,72... | collective-permute-start | bytes 2015240 | tf_op jit(solution)/shard_map/ppermute | solution.py:406
  22.9 9.0 %collective-permute-start.1 = (f32[8,5248]{1,0:T(8,128)S(1)}, f32[8,5248]{1,0:T(8,128)S(1)}, u32[]{:S(2)}, u32[]{:S(2)}) collective-permute-start(f32[8,5248]{1,0:T(8,128)S(1)} %get-tuple-element.21), channel_id=1, source_target_pairs={{0,32},{8,136},{16,48},{24,152},{32,0},{40,168},{48,16},{56,184},{... | collective-permute-start | bytes 503816 | tf_op jit(solution)/shard_map/ppermute | solution.py:413
  29.0 8.4 %collective-permute-start.3 = (f32[8,5248]{1,0:T(8,128)S(1)}, f32[8,5248]{1,0:T(8,128)S(1)}, u32[]{:S(2)}, u32[]{:S(2)}) collective-permute-start(f32[8,5248]{1,0:T(8,128)S(1)} %get-tuple-element.22), channel_id=1, source_target_pairs={{0,48},{8,200},{16,0},{24,216},{32,16},{40,232},{48,32},{56,248},{... | collective-permute-start | bytes 503816 | tf_op jit(solution)/shard_map/ppermute | solution.py:413
  29.2 8.1 %collective-permute-start.2 = (f32[8,5248]{1,0:T(8,128)S(1)}, f32[8,5248]{1,0:T(8,128)S(1)}, u32[]{:S(2)}, u32[]{:S(2)}) collective-permute-start(f32[8,5248]{1,0:T(8,128)S(1)} %get-tuple-element.23), channel_id=1, source_target_pairs={{0,16},{8,72},{16,32},{24,88},{32,48},{40,104},{48,0},{56,120},{64... | collective-permute-start | bytes 503816 | tf_op jit(solution)/shard_map/ppermute | solution.py:413
  37.4 4.8 %collective-permute-start.6 = (f32[2,5248]{1,0:T(2,128)S(1)}, f32[2,5248]{1,0:T(2,128)S(1)}, u32[]{:S(2)}, u32[]{:S(2)}) collective-permute-start(f32[2,5248]{1,0:T(2,128)S(1)} %get-tuple-element.24), channel_id=1, source_target_pairs={{0,192},{8,56},{16,208},{24,8},{32,224},{40,24},{48,240},{56,40},{... | collective-permute-start | bytes 125960 | tf_op jit(solution)/shard_map/ppermute | solution.py:413
  40.5 4.8 %collective-permute-start.5 = (f32[2,5248]{1,0:T(2,128)S(1)}, f32[2,5248]{1,0:T(2,128)S(1)}, u32[]{:S(2)}, u32[]{:S(2)}) collective-permute-start(f32[2,5248]{1,0:T(2,128)S(1)} %get-tuple-element.25), channel_id=1, source_target_pairs={{0,64},{8,24},{16,80},{24,40},{32,96},{40,56},{48,112},{56,8},{64,... | collective-permute-start | bytes 125960 | tf_op jit(solution)/shard_map/ppermute | solution.py:413
  40.5 4.8 %collective-permute-start.4 = (f32[2,5248]{1,0:T(2,128)S(1)}, f32[2,5248]{1,0:T(2,128)S(1)}, u32[]{:S(2)}, u32[]{:S(2)}) collective-permute-start(f32[2,5248]{1,0:T(2,128)S(1)} %get-tuple-element.26), channel_id=1, source_target_pairs={{0,128},{8,40},{16,144},{24,56},{32,160},{40,8},{48,176},{56,24},{... | collective-permute-start | bytes 125960 | tf_op jit(solution)/shard_map/ppermute | solution.py:413

commit v5 on v4

--- a/solution.py
+++ b/solution.py
@@ -123,8 +123,8 @@
     in_row = lax.broadcasted_iota(jnp.int32, (KDEV, KDEV), 1)
     to_core = jnp.where(out_row < 32, 1 - core, core)
     near, later = out_row >> 3, out_row >> 1
-    to_x = (x + jnp.where(to_core == 0, near, later)) & 3
-    to_z = (z + jnp.where(to_core == 0, later, near)) & 3
+    to_x = x ^ (jnp.where(to_core == 0, near, later) & 3)
+    to_z = z ^ (jnp.where(to_core == 0, later, near) & 3)
     order = in_row == to_z * 16 + to_x * 4 + to_core * 2 + (out_row & 1)
     order = jnp.where(order, 1.0, 0.0).astype(bf16)
 
@@ -408,15 +408,14 @@
     def step(value, d, stage):
         pairs = []
         for i in range(count):
-            along_x = (i // 8) * 8 + ((i // 2 + d) % 4) * 2 + i % 2
-            pairs.append((i, along_x if i % 2 == stage else (i + 8 * d) % count))
+            pairs.append((i, i ^ (2 * d if i % 2 == stage else 8 * d)))
         return lax.ppermute(value, "img", pairs)
 
     quarter = half[:8]
     for d in (2, 1, 3):
         quarter = quarter + step(half[8 * d : 8 * d + 8], d, 0)
     parts = [quarter[:2]]
-    for d in (2, 1, 3):
+    for d in (1, 3, 2):
         parts.append(step(quarter[2 * d : 2 * d + 2], d, 1))
     class_sums, ctf_sums = pl.pallas_call(
         last_kernel,

time: 46.4 us -> 45.6 us (0.983)
  starting transfers between devices: 15.4 us -> 13.2 us
  waiting for transfers between devices: 9.51 us -> 10.9 us
    ppermute x6, starting transfers between devices: 13.2 us -> 11 us  [step(): return lax.ppermute(value, 'img', pairs)]
    ppermute x6, waiting for transfers between devices: 9.09 us -> 10.5 us  [step(): return lax.ppermute(value, 'img', pairs)]
  transfers between devices with their start and end apart: 7 -> 7, of which waited for: 4 -> 6; matrix products, arithmetic and copies ran while one was open for 0% -> 0% of each run, Pallas kernels for 3% -> 3%
where the time goes in v5:
time: 45.6 us; the launch traced here: 45.4 us
  starting transfers between devices  13.2 us (29%)
  blocking collectives  11.2 us (25%)
  waiting for transfers between devices  10.9 us (24%)
  Pallas kernels  9.22 us (20%)
  between operations  0.67 us (1%)
    all_to_all x1, blocking collectives, on_device(): gathered = lax.all_to_all(stats, 'cls', 0, 0)  11.2 us
    ppermute x6, starting transfers between devices, step(): return lax.ppermute(value, 'img', pairs)  11 us
    ppermute x6, waiting for transfers between devices, step(): return lax.ppermute(value, 'img', pairs)  10.5 us
    pallas_call x1, Pallas kernels, on_device(): pl.pallas_call(score_kernel, out_shape=(shape(ROWS, COLS), shape(IMGS, FU...  6.02 us
    pallas_call x2, Pallas kernels, on_device(): pl.pallas_call(functools.partial(sum_kernel, first), out_shape=[shape(KDE...  2.23 us
    ppermute x1, starting transfers between devices, on_device(): half = keep + lax.ppermute(send, 'img', over_core)  2.2 us
    pallas_call x1, Pallas kernels, on_device(): pl.pallas_call(last_kernel, out_shape=(shape(2, FULL), shape(2, PLANE)),...  0.96 us
  transfers between devices with their start and end apart: 7, of which 6 were waited for; matrix products, arithmetic and copies ran while one was open for 0% of the time, Pallas kernels for 3%

profile of v5, /device:TPU:1, one launch (start us, length us, event | category | flops | bytes accessed | tf_op | source)
XLA Modules:
  0.0 45.4 jit_solution(4267557436427459460)
XLA Ops:
  0.6 6.0 %scores.1 = (f32[576,256]{1,0:T(8,128)S(1)}, bf16[64,4608]{1,0:T(8,128)(2,1)S(1)}, f32[8,2,128]{2,1,0:T(2,128)S(1)}, bf16[128,2304]{1,0:T(8,128)(2,1)S(1)}, s32[1,64]{1,0:T(1,128)S(1)}) custom-call(bf16[64,4608]{1,0:T(8,128)(2,1)} %images_hbm.1, bf16[64,4608]{1,0:T(8,128)(2,1)} %references_hbm.1, s32[2,64]{1,0:T(2,128)} %bitcast.4, s32[1,64]{1,0:T(1,128)} %bitcast.5, ...), custom_call_target="tpu_custom_call" | custom-call | tf_op jit(solution)/shard_map/scores/pallas_call | solution.py:364
  6.7 11.2 %all_to_all.5.stats_ref = f32[8,2,128]{2,1,0:T(2,128)S(1)} all-to-all(f32[8,2,128]{2,1,0:T(2,128)S(1)} %get-tuple-element.12.mine_ref), channel_id=1, replica_groups=mesh['img'=32,'cls'=8] {'cls'}, dimensions={0} | all-to-all | bytes 16384 | tf_op jit(solution)/shard_map/all_to_all | solution.py:388
  17.9 0.9 %sums.3 = f32[32,5248]{1,0:T(8,128)S(1)} custom-call(f32[8,2,128]{2,1,0:T(2,128)S(1)} %all_to_all.5.stats_ref, f32[8,2,128]{2,1,0:T(2,128)S(1)} %get-tuple-element.12.mine_ref, f32[576,256]{1,0:T(8,128)S(1)} %get-tuple-element.13.expo_ref, bf16[64,4608]{1,0:T(8,128)(2,1)S(1)} %get-tuple-element.14.weighted_ref, s32[1,64]{1,0:T(1,128)S(1)} %get-tuple-element.15.groups_ref), custom_call_target="tpu_custom_call" | custom-call | flops 679477248 | bytes 294912 | tf_op jit(solution)/shard_map/sums/pallas_call | solution.py:392
  18.8 2.2 %collective-permute-start = (f32[32,5248]{1,0:T(8,128)S(1)}, f32[32,5248]{1,0:T(8,128)S(1)}, u32[]{:S(2)}, u32[]{:S(2)}) collective-permute-start(f32[32,5248]{1,0:T(8,128)S(1)} %sums.3), channel_id=1, source_target_pairs={{0,8},{8,0},{16,24},{24,16},{32,40},{40,32},{48,56},{56,48},{64,72... | collective-permute-start | bytes 2015240 | tf_op jit(solution)/shard_map/ppermute | solution.py:406
  21.0 1.3 %sums.2 = (f32[32,5248]{1,0:T(8,128)S(1)}, f32[1,64]{1,0:T(1,128)}) custom-call(f32[8,2,128]{2,1,0:T(2,128)S(1)} %all_to_all.5.stats_ref, f32[8,2,128]{2,1,0:T(2,128)S(1)} %get-tuple-element.12.mine_ref, f32[576,256]{1,0:T(8,128)S(1)} %get-tuple-element.13.expo_ref, bf16[64,4608]{1,0:T(8,128)(2,1)S(1)} %get-tuple-element.14.weighted_ref, ...), custom_call_target="tpu_custom_call" | custom-call | flops 679477248 | bytes 294912 | tf_op jit(solution)/shard_map/sums/pallas_call | solution.py:392
  22.3 0.4 collective-permute-done
  22.7 0.1 add.12
  22.9 6.1 %collective-permute-start.1 = (f32[8,5248]{1,0:T(8,128)S(1)}, f32[8,5248]{1,0:T(8,128)S(1)}, u32[]{:S(2)}, u32[]{:S(2)}) collective-permute-start(f32[8,5248]{1,0:T(8,128)S(1)} %get-tuple-element.21), channel_id=1, source_target_pairs={{0,32},{8,136},{16,48},{24,152},{32,0},{40,168},{48,16},{56,184},{... | collective-permute-start | bytes 503816 | tf_op jit(solution)/shard_map/ppermute | solution.py:412
  29.0 0.3 collective-permute-start.3
  29.2 0.9 %collective-permute-start.2 = (f32[8,5248]{1,0:T(8,128)S(1)}, f32[8,5248]{1,0:T(8,128)S(1)}, u32[]{:S(2)}, u32[]{:S(2)}) collective-permute-start(f32[8,5248]{1,0:T(8,128)S(1)} %get-tuple-element.23), channel_id=1, source_target_pairs={{0,16},{8,72},{16,0},{24,88},{32,48},{40,104},{48,32},{56,120},{64... | collective-permute-start | bytes 503816 | tf_op jit(solution)/shard_map/ppermute | solution.py:412
  30.2 1.7 %collective-permute-done.1 = f32[8,5248]{1,0:T(8,128)S(1)} collective-permute-done((f32[8,5248]{1,0:T(8,128)S(1)}, f32[8,5248]{1,0:T(8,128)S(1)}, u32[]{:S(2)}, u32[]{:S(2)}) %collective-permute-start.1) | collective-permute-done | bytes 167968 | tf_op jit(solution)/shard_map/ppermute | solution.py:412
  31.8 4.7 %collective-permute-done.3 = f32[8,5248]{1,0:T(8,128)S(1)} collective-permute-done((f32[8,5248]{1,0:T(8,128)S(1)}, f32[8,5248]{1,0:T(8,128)S(1)}, u32[]{:S(2)}, u32[]{:S(2)}) %collective-permute-start.3) | collective-permute-done | bytes 167968 | tf_op jit(solution)/shard_map/ppermute | solution.py:412
  36.5 0.8 %collective-permute-done.2 = f32[8,5248]{1,0:T(8,128)S(1)} collective-permute-done((f32[8,5248]{1,0:T(8,128)S(1)}, f32[8,5248]{1,0:T(8,128)S(1)}, u32[]{:S(2)}, u32[]{:S(2)}) %collective-permute-start.2) | collective-permute-done | bytes 167968 | tf_op jit(solution)/shard_map/ppermute | solution.py:412
  37.4 0.1 fusion.3
  37.4 2.8 %collective-permute-start.6 = (f32[2,5248]{1,0:T(2,128)S(1)}, f32[2,5248]{1,0:T(2,128)S(1)}, u32[]{:S(2)}, u32[]{:S(2)}) collective-permute-start(f32[2,5248]{1,0:T(2,128)S(1)} %get-tuple-element.24), channel_id=1, source_target_pairs={{0,128},{8,40},{16,144},{24,56},{32,160},{40,8},{48,176},{56,24},{... | collective-permute-start | bytes 125960 | tf_op jit(solution)/shard_map/ppermute | solution.py:412
  40.3 0.9 %collective-permute-start.5 = (f32[2,5248]{1,0:T(2,128)S(1)}, f32[2,5248]{1,0:T(2,128)S(1)}, u32[]{:S(2)}, u32[]{:S(2)}) collective-permute-start(f32[2,5248]{1,0:T(2,128)S(1)} %get-tuple-element.25), channel_id=1, source_target_pairs={{0,192},{8,56},{16,208},{24,40},{32,224},{40,24},{48,240},{56,8},{... | collective-permute-start | bytes 125960 | tf_op jit(solution)/shard_map/ppermute | solution.py:412
  41.1 0.0 collective-permute-start.4
  41.1 0.8 %collective-permute-done.6.d_ref = f32[2,5248]{1,0:T(2,128)S(1)} collective-permute-done((f32[2,5248]{1,0:T(2,128)S(1)}, f32[2,5248]{1,0:T(2,128)S(1)}, u32[]{:S(2)}, u32[]{:S(2)}) %collective-permute-start.6) | collective-permute-done | bytes 42016 | tf_op jit(solution)/shard_map/ppermute | solution.py:412
  41.9 2.6 %collective-permute-done.5.c_ref = f32[2,5248]{1,0:T(2,128)S(1)} collective-permute-done((f32[2,5248]{1,0:T(2,128)S(1)}, f32[2,5248]{1,0:T(2,128)S(1)}, u32[]{:S(2)}, u32[]{:S(2)}) %collective-permute-start.5) | collective-permute-done | bytes 42016 | tf_op jit(solution)/shard_map/ppermute | solution.py:412
  44.5 0.0 collective-permute-done.4.b_ref
  44.5 1.0 %ctf.1 = (f32[2,4608]{1,0:T(2,128)}, f32[2,2304]{1,0:T(2,128)}) custom-call(f32[2,5248]{1,0:T(2,128)S(1)} %get-tuple-element.27.a_ref, f32[2,5248]{1,0:T(2,128)S(1)} %collective-permute-done.4.b_ref, f32[2,5248]{1,0:T(2,128)S(1)} %collective-permute-done.5.c_ref, f32[2,5248]{1,0:T(2,128)S(1)} %collective-permute-done.6.d_ref, ...), custom_call_target="tpu_custom_call" | custom-call | tf_op jit(solution)/shard_map/ctf/pallas_call | solution.py:420
  (2 shorter events, 0.1 us)
Async XLA Ops:
  18.8 3.9 %collective-permute-start = (f32[32,5248]{1,0:T(8,128)S(1)}, f32[32,5248]{1,0:T(8,128)S(1)}, u32[]{:S(2)}, u32[]{:S(2)}) collective-permute-start(f32[32,5248]{1,0:T(8,128)S(1)} %sums.3), channel_id=1, source_target_pairs={{0,8},{8,0},{16,24},{24,16},{32,40},{40,32},{48,56},{56,48},{64,72... | collective-permute-start | bytes 2015240 | tf_op jit(solution)/shard_map/ppermute | solution.py:406
  22.9 9.0 %collective-permute-start.1 = (f32[8,5248]{1,0:T(8,128)S(1)}, f32[8,5248]{1,0:T(8,128)S(1)}, u32[]{:S(2)}, u32[]{:S(2)}) collective-permute-start(f32[8,5248]{1,0:T(8,128)S(1)} %get-tuple-element.21), channel_id=1, source_target_pairs={{0,32},{8,136},{16,48},{24,152},{32,0},{40,168},{48,16},{56,184},{... | collective-permute-start | bytes 503816 | tf_op jit(solution)/shard_map/ppermute | solution.py:412
  29.0 7.6 %collective-permute-start.3 = (f32[8,5248]{1,0:T(8,128)S(1)}, f32[8,5248]{1,0:T(8,128)S(1)}, u32[]{:S(2)}, u32[]{:S(2)}) collective-permute-start(f32[8,5248]{1,0:T(8,128)S(1)} %get-tuple-element.22), channel_id=1, source_target_pairs={{0,48},{8,200},{16,32},{24,216},{32,16},{40,232},{48,0},{56,248},{... | collective-permute-start | bytes 503816 | tf_op jit(solution)/shard_map/ppermute | solution.py:412
  29.2 8.1 %collective-permute-start.2 = (f32[8,5248]{1,0:T(8,128)S(1)}, f32[8,5248]{1,0:T(8,128)S(1)}, u32[]{:S(2)}, u32[]{:S(2)}) collective-permute-start(f32[8,5248]{1,0:T(8,128)S(1)} %get-tuple-element.23), channel_id=1, source_target_pairs={{0,16},{8,72},{16,0},{24,88},{32,48},{40,104},{48,32},{56,120},{64... | collective-permute-start | bytes 503816 | tf_op jit(solution)/shard_map/ppermute | solution.py:412
  37.4 4.5 %collective-permute-start.6 = (f32[2,5248]{1,0:T(2,128)S(1)}, f32[2,5248]{1,0:T(2,128)S(1)}, u32[]{:S(2)}, u32[]{:S(2)}) collective-permute-start(f32[2,5248]{1,0:T(2,128)S(1)} %get-tuple-element.24), channel_id=1, source_target_pairs={{0,128},{8,40},{16,144},{24,56},{32,160},{40,8},{48,176},{56,24},{... | collective-permute-start | bytes 125960 | tf_op jit(solution)/shard_map/ppermute | solution.py:412
  40.3 4.2 %collective-permute-start.5 = (f32[2,5248]{1,0:T(2,128)S(1)}, f32[2,5248]{1,0:T(2,128)S(1)}, u32[]{:S(2)}, u32[]{:S(2)}) collective-permute-start(f32[2,5248]{1,0:T(2,128)S(1)} %get-tuple-element.25), channel_id=1, source_target_pairs={{0,192},{8,56},{16,208},{24,40},{32,224},{40,24},{48,240},{56,8},{... | collective-permute-start | bytes 125960 | tf_op jit(solution)/shard_map/ppermute | solution.py:412
  41.1 3.4 %collective-permute-start.4 = (f32[2,5248]{1,0:T(2,128)S(1)}, f32[2,5248]{1,0:T(2,128)S(1)}, u32[]{:S(2)}, u32[]{:S(2)}) collective-permute-start(f32[2,5248]{1,0:T(2,128)S(1)} %get-tuple-element.26), channel_id=1, source_target_pairs={{0,64},{8,24},{16,80},{24,8},{32,96},{40,56},{48,112},{56,40},{64,... | collective-permute-start | bytes 125960 | tf_op jit(solution)/shard_map/ppermute | solution.py:412

commit v6 on v5

--- a/solution.py
+++ b/solution.py
@@ -415,7 +415,7 @@
     for d in (2, 1, 3):
         quarter = quarter + step(half[8 * d : 8 * d + 8], d, 0)
     parts = [quarter[:2]]
-    for d in (1, 3, 2):
+    for d in (1, 2, 3):
         parts.append(step(quarter[2 * d : 2 * d + 2], d, 1))
     class_sums, ctf_sums = pl.pallas_call(
         last_kernel,

time: 45.6 us -> 45.5 us (level)
  no operation moved by 1% of the time
where the time goes in v6:
time: 45.5 us; the launch traced here: 45.3 us
  starting transfers between devices  12.8 us (28%)
  blocking collectives  11.2 us (25%)
  waiting for transfers between devices  11.2 us (25%)
  Pallas kernels  9.22 us (20%)
  between operations  0.67 us (1%)
    all_to_all x1, blocking collectives, on_device(): gathered = lax.all_to_all(stats, 'cls', 0, 0)  11.2 us
    ppermute x6, waiting for transfers between devices, step(): return lax.ppermute(value, 'img', pairs)  10.8 us
    ppermute x6, starting transfers between devices, step(): return lax.ppermute(value, 'img', pairs)  10.6 us
    pallas_call x1, Pallas kernels, on_device(): pl.pallas_call(score_kernel, out_shape=(shape(ROWS, COLS), shape(IMGS, FU...  6.02 us
    pallas_call x2, Pallas kernels, on_device(): pl.pallas_call(functools.partial(sum_kernel, first), out_shape=[shape(KDE...  2.23 us
    ppermute x1, starting transfers between devices, on_device(): half = keep + lax.ppermute(send, 'img', over_core)  2.2 us
    pallas_call x1, Pallas kernels, on_device(): pl.pallas_call(last_kernel, out_shape=(shape(2, FULL), shape(2, PLANE)),...  0.97 us
  transfers between devices with their start and end apart: 7, of which 6 were waited for; matrix products, arithmetic and copies ran while one was open for 0% of the time, Pallas kernels for 3%

profile of v6, /device:TPU:1, one launch (start us, length us, event | category | flops | bytes accessed | tf_op | source)
XLA Modules:
  0.0 45.3 jit_solution(16206458247128642284)
XLA Ops:
  0.6 6.0 %scores.1 = (f32[576,256]{1,0:T(8,128)S(1)}, bf16[64,4608]{1,0:T(8,128)(2,1)S(1)}, f32[8,2,128]{2,1,0:T(2,128)S(1)}, bf16[128,2304]{1,0:T(8,128)(2,1)S(1)}, s32[1,64]{1,0:T(1,128)S(1)}) custom-call(bf16[64,4608]{1,0:T(8,128)(2,1)} %images_hbm.1, bf16[64,4608]{1,0:T(8,128)(2,1)} %references_hbm.1, s32[2,64]{1,0:T(2,128)} %bitcast.4, s32[1,64]{1,0:T(1,128)} %bitcast.5, ...), custom_call_target="tpu_custom_call" | custom-call | tf_op jit(solution)/shard_map/scores/pallas_call | solution.py:364
  6.7 11.2 %all_to_all.5.stats_ref = f32[8,2,128]{2,1,0:T(2,128)S(1)} all-to-all(f32[8,2,128]{2,1,0:T(2,128)S(1)} %get-tuple-element.12.mine_ref), channel_id=1, replica_groups=mesh['img'=32,'cls'=8] {'cls'}, dimensions={0} | all-to-all | bytes 16384 | tf_op jit(solution)/shard_map/all_to_all | solution.py:388
  17.9 0.9 %sums.3 = f32[32,5248]{1,0:T(8,128)S(1)} custom-call(f32[8,2,128]{2,1,0:T(2,128)S(1)} %all_to_all.5.stats_ref, f32[8,2,128]{2,1,0:T(2,128)S(1)} %get-tuple-element.12.mine_ref, f32[576,256]{1,0:T(8,128)S(1)} %get-tuple-element.13.expo_ref, bf16[64,4608]{1,0:T(8,128)(2,1)S(1)} %get-tuple-element.14.weighted_ref, s32[1,64]{1,0:T(1,128)S(1)} %get-tuple-element.15.groups_ref), custom_call_target="tpu_custom_call" | custom-call | flops 679477248 | bytes 294912 | tf_op jit(solution)/shard_map/sums/pallas_call | solution.py:392
  18.8 2.2 %collective-permute-start = (f32[32,5248]{1,0:T(8,128)S(1)}, f32[32,5248]{1,0:T(8,128)S(1)}, u32[]{:S(2)}, u32[]{:S(2)}) collective-permute-start(f32[32,5248]{1,0:T(8,128)S(1)} %sums.3), channel_id=1, source_target_pairs={{0,8},{8,0},{16,24},{24,16},{32,40},{40,32},{48,56},{56,48},{64,72... | collective-permute-start | bytes 2015240 | tf_op jit(solution)/shard_map/ppermute | solution.py:406
  21.0 1.3 %sums.2 = (f32[32,5248]{1,0:T(8,128)S(1)}, f32[1,64]{1,0:T(1,128)}) custom-call(f32[8,2,128]{2,1,0:T(2,128)S(1)} %all_to_all.5.stats_ref, f32[8,2,128]{2,1,0:T(2,128)S(1)} %get-tuple-element.12.mine_ref, f32[576,256]{1,0:T(8,128)S(1)} %get-tuple-element.13.expo_ref, bf16[64,4608]{1,0:T(8,128)(2,1)S(1)} %get-tuple-element.14.weighted_ref, ...), custom_call_target="tpu_custom_call" | custom-call | flops 679477248 | bytes 294912 | tf_op jit(solution)/shard_map/sums/pallas_call | solution.py:392
  22.3 0.4 collective-permute-done
  22.7 0.1 add.12
  22.9 6.1 %collective-permute-start.1 = (f32[8,5248]{1,0:T(8,128)S(1)}, f32[8,5248]{1,0:T(8,128)S(1)}, u32[]{:S(2)}, u32[]{:S(2)}) collective-permute-start(f32[8,5248]{1,0:T(8,128)S(1)} %get-tuple-element.21), channel_id=1, source_target_pairs={{0,32},{8,136},{16,48},{24,152},{32,0},{40,168},{48,16},{56,184},{... | collective-permute-start | bytes 503816 | tf_op jit(solution)/shard_map/ppermute | solution.py:412
  29.0 0.3 collective-permute-start.3
  29.2 0.9 %collective-permute-start.2 = (f32[8,5248]{1,0:T(8,128)S(1)}, f32[8,5248]{1,0:T(8,128)S(1)}, u32[]{:S(2)}, u32[]{:S(2)}) collective-permute-start(f32[8,5248]{1,0:T(8,128)S(1)} %get-tuple-element.23), channel_id=1, source_target_pairs={{0,16},{8,72},{16,0},{24,88},{32,48},{40,104},{48,32},{56,120},{64... | collective-permute-start | bytes 503816 | tf_op jit(solution)/shard_map/ppermute | solution.py:412
  30.2 1.7 %collective-permute-done.1 = f32[8,5248]{1,0:T(8,128)S(1)} collective-permute-done((f32[8,5248]{1,0:T(8,128)S(1)}, f32[8,5248]{1,0:T(8,128)S(1)}, u32[]{:S(2)}, u32[]{:S(2)}) %collective-permute-start.1) | collective-permute-done | bytes 167968 | tf_op jit(solution)/shard_map/ppermute | solution.py:412
  31.8 4.7 %collective-permute-done.3 = f32[8,5248]{1,0:T(8,128)S(1)} collective-permute-done((f32[8,5248]{1,0:T(8,128)S(1)}, f32[8,5248]{1,0:T(8,128)S(1)}, u32[]{:S(2)}, u32[]{:S(2)}) %collective-permute-start.3) | collective-permute-done | bytes 167968 | tf_op jit(solution)/shard_map/ppermute | solution.py:412
  36.5 0.8 %collective-permute-done.2 = f32[8,5248]{1,0:T(8,128)S(1)} collective-permute-done((f32[8,5248]{1,0:T(8,128)S(1)}, f32[8,5248]{1,0:T(8,128)S(1)}, u32[]{:S(2)}, u32[]{:S(2)}) %collective-permute-start.2) | collective-permute-done | bytes 167968 | tf_op jit(solution)/shard_map/ppermute | solution.py:412
  37.4 0.1 fusion.3
  37.4 2.6 %collective-permute-start.6 = (f32[2,5248]{1,0:T(2,128)S(1)}, f32[2,5248]{1,0:T(2,128)S(1)}, u32[]{:S(2)}, u32[]{:S(2)}) collective-permute-start(f32[2,5248]{1,0:T(2,128)S(1)} %get-tuple-element.24), channel_id=1, source_target_pairs={{0,192},{8,56},{16,208},{24,40},{32,224},{40,24},{48,240},{56,8},{... | collective-permute-start | bytes 125960 | tf_op jit(solution)/shard_map/ppermute | solution.py:412
  40.0 0.5 %collective-permute-start.5 = (f32[2,5248]{1,0:T(2,128)S(1)}, f32[2,5248]{1,0:T(2,128)S(1)}, u32[]{:S(2)}, u32[]{:S(2)}) collective-permute-start(f32[2,5248]{1,0:T(2,128)S(1)} %get-tuple-element.25), channel_id=1, source_target_pairs={{0,128},{8,40},{16,144},{24,56},{32,160},{40,8},{48,176},{56,24},{... | collective-permute-start | bytes 125960 | tf_op jit(solution)/shard_map/ppermute | solution.py:412
  40.5 0.3 collective-permute-start.4
  40.8 0.8 %collective-permute-done.6.d_ref = f32[2,5248]{1,0:T(2,128)S(1)} collective-permute-done((f32[2,5248]{1,0:T(2,128)S(1)}, f32[2,5248]{1,0:T(2,128)S(1)}, u32[]{:S(2)}, u32[]{:S(2)}) %collective-permute-start.6) | collective-permute-done | bytes 42016 | tf_op jit(solution)/shard_map/ppermute | solution.py:412
  41.6 2.8 %collective-permute-done.5.c_ref = f32[2,5248]{1,0:T(2,128)S(1)} collective-permute-done((f32[2,5248]{1,0:T(2,128)S(1)}, f32[2,5248]{1,0:T(2,128)S(1)}, u32[]{:S(2)}, u32[]{:S(2)}) %collective-permute-start.5) | collective-permute-done | bytes 42016 | tf_op jit(solution)/shard_map/ppermute | solution.py:412
  44.4 0.0 collective-permute-done.4.b_ref
  44.4 1.0 %ctf.1 = (f32[2,4608]{1,0:T(2,128)}, f32[2,2304]{1,0:T(2,128)}) custom-call(f32[2,5248]{1,0:T(2,128)S(1)} %get-tuple-element.27.a_ref, f32[2,5248]{1,0:T(2,128)S(1)} %collective-permute-done.4.b_ref, f32[2,5248]{1,0:T(2,128)S(1)} %collective-permute-done.5.c_ref, f32[2,5248]{1,0:T(2,128)S(1)} %collective-permute-done.6.d_ref, ...), custom_call_target="tpu_custom_call" | custom-call | tf_op jit(solution)/shard_map/ctf/pallas_call | solution.py:420
  (2 shorter events, 0.1 us)
Async XLA Ops:
  18.8 3.9 %collective-permute-start = (f32[32,5248]{1,0:T(8,128)S(1)}, f32[32,5248]{1,0:T(8,128)S(1)}, u32[]{:S(2)}, u32[]{:S(2)}) collective-permute-start(f32[32,5248]{1,0:T(8,128)S(1)} %sums.3), channel_id=1, source_target_pairs={{0,8},{8,0},{16,24},{24,16},{32,40},{40,32},{48,56},{56,48},{64,72... | collective-permute-start | bytes 2015240 | tf_op jit(solution)/shard_map/ppermute | solution.py:406
  22.9 9.0 %collective-permute-start.1 = (f32[8,5248]{1,0:T(8,128)S(1)}, f32[8,5248]{1,0:T(8,128)S(1)}, u32[]{:S(2)}, u32[]{:S(2)}) collective-permute-start(f32[8,5248]{1,0:T(8,128)S(1)} %get-tuple-element.21), channel_id=1, source_target_pairs={{0,32},{8,136},{16,48},{24,152},{32,0},{40,168},{48,16},{56,184},{... | collective-permute-start | bytes 503816 | tf_op jit(solution)/shard_map/ppermute | solution.py:412
  29.0 7.6 %collective-permute-start.3 = (f32[8,5248]{1,0:T(8,128)S(1)}, f32[8,5248]{1,0:T(8,128)S(1)}, u32[]{:S(2)}, u32[]{:S(2)}) collective-permute-start(f32[8,5248]{1,0:T(8,128)S(1)} %get-tuple-element.22), channel_id=1, source_target_pairs={{0,48},{8,200},{16,32},{24,216},{32,16},{40,232},{48,0},{56,248},{... | collective-permute-start | bytes 503816 | tf_op jit(solution)/shard_map/ppermute | solution.py:412
  29.2 8.1 %collective-permute-start.2 = (f32[8,5248]{1,0:T(8,128)S(1)}, f32[8,5248]{1,0:T(8,128)S(1)}, u32[]{:S(2)}, u32[]{:S(2)}) collective-permute-start(f32[8,5248]{1,0:T(8,128)S(1)} %get-tuple-element.23), channel_id=1, source_target_pairs={{0,16},{8,72},{16,0},{24,88},{32,48},{40,104},{48,32},{56,120},{64... | collective-permute-start | bytes 503816 | tf_op jit(solution)/shard_map/ppermute | solution.py:412
  37.4 4.2 %collective-permute-start.6 = (f32[2,5248]{1,0:T(2,128)S(1)}, f32[2,5248]{1,0:T(2,128)S(1)}, u32[]{:S(2)}, u32[]{:S(2)}) collective-permute-start(f32[2,5248]{1,0:T(2,128)S(1)} %get-tuple-element.24), channel_id=1, source_target_pairs={{0,192},{8,56},{16,208},{24,40},{32,224},{40,24},{48,240},{56,8},{... | collective-permute-start | bytes 125960 | tf_op jit(solution)/shard_map/ppermute | solution.py:412
  40.0 4.4 %collective-permute-start.5 = (f32[2,5248]{1,0:T(2,128)S(1)}, f32[2,5248]{1,0:T(2,128)S(1)}, u32[]{:S(2)}, u32[]{:S(2)}) collective-permute-start(f32[2,5248]{1,0:T(2,128)S(1)} %get-tuple-element.25), channel_id=1, source_target_pairs={{0,128},{8,40},{16,144},{24,56},{32,160},{40,8},{48,176},{56,24},{... | collective-permute-start | bytes 125960 | tf_op jit(solution)/shard_map/ppermute | solution.py:412
  40.5 3.9 %collective-permute-start.4 = (f32[2,5248]{1,0:T(2,128)S(1)}, f32[2,5248]{1,0:T(2,128)S(1)}, u32[]{:S(2)}, u32[]{:S(2)}) collective-permute-start(f32[2,5248]{1,0:T(2,128)S(1)} %get-tuple-element.26), channel_id=1, source_target_pairs={{0,64},{8,24},{16,80},{24,8},{32,96},{40,56},{48,112},{56,40},{64,... | collective-permute-start | bytes 125960 | tf_op jit(solution)/shard_map/ppermute | solution.py:412
